TPU v7x, 32 devices: a whole 2x2x4 slice. The times are simulated.
32 devices in a mesh: dp: 8 (over z, y), tensor: 4 (over x, core).
Axes of the slice: x: 2, y: 2, z: 4, core: 2. Of those that a mesh axis runs over, the one named last changes fastest.
Arguments:
- tokens: bfloat16 [7680, 1024], P('dp'), may hold values from -6 to 6
- kept: int32 [24], replicated, may hold values from 192 to 256, as said below
- teacher: bfloat16 [7680, 1024], P('dp'), may hold values from -6 to 6
- out_grad: bfloat16 [7680, 1024], P('dp'), may hold values from -6 to 6
- ln1_gain: bfloat16 [1024], replicated, may hold values from 0.5 to 1.5
- ln1_bias: bfloat16 [1024], replicated, may hold values from -0.3125 to 0.3125
- w_qkv: bfloat16 [1024, 3, 1024], P(None, None, 'tensor'), may hold values from -0.1875 to 0.1875
- bias_qv: bfloat16 [2, 1024], P(None, 'tensor'), may hold values from -0.3125 to 0.3125
- w_proj: bfloat16 [1024, 1024], P('tensor'), may hold values from -1 to 1
- bias_proj: bfloat16 [1024], replicated, may hold values from -0.625 to 0.625
- ln2_gain: bfloat16 [1024], replicated, may hold values from 0.5 to 1.5
- ln2_bias: bfloat16 [1024], replicated, may hold values from -1.75 to 1.75
- w_fc1: bfloat16 [1024, 4096], P(None, 'tensor'), may hold values from -0.1875 to 0.1875
- bias_fc1: bfloat16 [4096], P('tensor'), may hold values from -0.625 to 0.625
- w_fc2: bfloat16 [4096, 1024], P('tensor'), may hold values from -0.09375 to 0.09375
- bias_fc2: bfloat16 [1024], replicated, may hold values from -0.625 to 0.625
Outputs:
- out: bfloat16 [7680, 1024], P('dp')
- loss: float32 [24], P('dp')
- token_grad: float32 [7680, 1024], P('dp')
- grad_ln1_gain: float32 [1024], replicated
- grad_ln1_bias: float32 [1024], replicated
- grad_w_qkv: float32 [1024, 3, 1024], P('dp', None, 'tensor')
- grad_bias_qv: float32 [2, 1024], P(None, 'tensor')
- grad_w_proj: float32 [1024, 1024], P('tensor', 'dp')
- grad_bias_proj: float32 [1024], replicated
- grad_ln2_gain: float32 [1024], replicated
- grad_ln2_bias: float32 [1024], replicated
- grad_w_fc1: float32 [1024, 4096], P('dp', 'tensor')
- grad_bias_fc1: float32 [4096], P('tensor')
- grad_w_fc2: float32 [4096, 1024], P('tensor', 'dp')
- grad_bias_fc2: float32 [1024], replicated
Inputs may be any that keep to these rules, and one draw needn't show every extreme that they name: The valid rows of sequence s are its 64 buffer slots and the next kept[s] slots; the remaining slots are padding.
All inputs are finite; a program needn't handle non-finite values.
Results may differ from a plain program's by a relative error of at most 0.014.
The roundings to bfloat16 on the way count: a program that leaves them out, or rounds other values in their place, can miss the bound.
Values may be sent and summed in bfloat16 or wider, within the bound.
A program may use at most 128 MiB of HBM per device.

v0:
```python
import jax
import jax.numpy as jnp
from jax import lax
from jax.sharding import PartitionSpec as P

D = 1024
H = 16
BUFFER = 64
SLOTS = 320


eps_norm = 1e-06


def norm_apply(hidden, norm_gain, norm_shift):
    center = jnp.mean(hidden, axis=-1, keepdims=True)
    offset = hidden - center
    spread = jnp.mean(offset * offset, axis=-1, keepdims=True)
    return offset * lax.rsqrt(spread + eps_norm) * norm_gain + norm_shift


def gelu_exact(values):
    return jax.nn.gelu(values, approximate=False)


def masked_scores(queries, key_rows, validity, score_scale):
    scores = (
        jnp.einsum("bshe,brhe->bhsr", queries, key_rows, preferred_element_type=jnp.float32)
        * score_scale
    )
    return jnp.where(validity[:, None, None, :] > 0, scores, -1e30)


def body(
    tokens,
    kept,
    teacher,
    out_grad,
    ln1_gain,
    ln1_bias,
    w_qkv,
    bias_qv,
    w_proj,
    bias_proj,
    ln2_gain,
    ln2_bias,
    w_fc1,
    bias_fc1,
    w_fc2,
    bias_fc2,
):
    row_count = tokens.shape[0]
    sequences = row_count // SLOTS
    all_seqs = kept.shape[0]
    local_width = w_qkv.shape[2]
    head_size = D // H
    head_count = local_width // head_size
    score_scale = head_size ** (-0.5)
    first_seq = lax.axis_index("dp") * sequences
    my_kept = lax.dynamic_slice_in_dim(kept, first_seq, sequences)
    slot_index = lax.iota(jnp.int32, SLOTS)
    validity = (slot_index[None, :] < (BUFFER + my_kept)[:, None]).astype(jnp.float32)
    row_mask = validity.reshape(row_count, 1)
    valid_count = jnp.sum((BUFFER + kept).astype(jnp.float32))
    masked_in = tokens.astype(jnp.float32) * row_mask
    normed, first_pull = jax.vjp(
        norm_apply, masked_in, ln1_gain.astype(jnp.float32), ln1_bias.astype(jnp.float32)
    )
    normed_low = normed.astype(jnp.bfloat16)
    bias_full = jnp.stack([bias_qv[0], jnp.zeros_like(bias_qv[0]), bias_qv[1]]).astype(jnp.float32)
    qkv_low = (
        jnp.einsum("td,dcf->tcf", normed_low, w_qkv, preferred_element_type=jnp.float32) + bias_full
    ).astype(jnp.bfloat16)
    head_shape = (sequences, SLOTS, head_count, head_size)
    queries = qkv_low[:, 0].reshape(head_shape)
    key_rows = qkv_low[:, 1].reshape(head_shape)
    value_rows = qkv_low[:, 2].reshape(head_shape)
    scores = masked_scores(queries, key_rows, validity, score_scale)
    top_score = jnp.max(scores, axis=-1, keepdims=True)
    log_total = top_score + jnp.log(jnp.sum(jnp.exp(scores - top_score), axis=-1, keepdims=True))
    probs_low = jnp.exp(scores - log_total).astype(jnp.bfloat16)
    head_out = jnp.einsum(
        "bhsr,brhe->bshe", probs_low, value_rows, preferred_element_type=jnp.float32
    )
    head_low = head_out.reshape(row_count, local_width).astype(jnp.bfloat16)
    attn_part = jnp.dot(head_low, w_proj, preferred_element_type=jnp.float32)
    attn_total = lax.psum(attn_part.astype(jnp.bfloat16), "tensor").astype(jnp.float32)
    resid_one = masked_in + attn_total + bias_proj.astype(jnp.float32)
    second, second_pull = jax.vjp(
        norm_apply, resid_one, ln2_gain.astype(jnp.float32), ln2_bias.astype(jnp.float32)
    )
    second_low = second.astype(jnp.bfloat16)
    pre_act = jnp.dot(second_low, w_fc1, preferred_element_type=jnp.float32) + bias_fc1.astype(
        jnp.float32
    )
    act_value, gelu_pull = jax.vjp(gelu_exact, pre_act)
    act_low = act_value.astype(jnp.bfloat16)
    mlp_part = jnp.dot(act_low, w_fc2, preferred_element_type=jnp.float32)
    mlp_total = lax.psum(mlp_part.astype(jnp.bfloat16), "tensor").astype(jnp.float32)
    final_out = (resid_one + mlp_total + bias_fc2.astype(jnp.float32)) * row_mask
    errors = (final_out - teacher.astype(jnp.float32)) * row_mask
    squared = errors * errors
    seq_sq = jnp.sum(squared.reshape(sequences, SLOTS * D), axis=1)
    loss_value = seq_sq * (all_seqs / (2.0 * valid_count * D))
    total_slots = all_seqs * SLOTS * 1.0
    seed_grad = (out_grad.astype(jnp.float32) + errors * (total_slots / valid_count)) * row_mask
    seed_low = seed_grad.astype(jnp.bfloat16)
    grad_bias_fc2 = jnp.sum(seed_grad, axis=0)
    grad_w_fc2 = jnp.einsum("tf,te->fe", act_low, seed_low, preferred_element_type=jnp.float32)
    d_act = jnp.einsum("te,fe->tf", seed_low, w_fc2, preferred_element_type=jnp.float32)
    d_pre_low = gelu_pull(d_act)[0].astype(jnp.bfloat16)
    grad_bias_fc1 = jnp.sum(d_pre_low, axis=0, dtype=jnp.float32)
    grad_w_fc1 = jnp.einsum("td,tf->df", second_low, d_pre_low, preferred_element_type=jnp.float32)
    d_second_part = jnp.einsum("tf,df->td", d_pre_low, w_fc1, preferred_element_type=jnp.float32)
    d_second = lax.psum(d_second_part.astype(jnp.bfloat16), "tensor").astype(jnp.float32)
    d_resid, grad_ln2_gain, grad_ln2_bias = second_pull(d_second)
    d_resid = d_resid + seed_grad
    grad_bias_proj = jnp.sum(d_resid, axis=0)
    d_attn_low = d_resid.astype(jnp.bfloat16)
    grad_w_proj = jnp.einsum("tf,te->fe", head_low, d_attn_low, preferred_element_type=jnp.float32)
    d_head_low = (
        jnp.einsum("te,fe->tf", d_attn_low, w_proj, preferred_element_type=jnp.float32)
        .astype(jnp.bfloat16)
        .reshape(head_shape)
    )
    scores_again = masked_scores(queries, key_rows, validity, score_scale)
    probs = jnp.exp(scores_again - log_total)
    grad_v = jnp.einsum(
        "bhsr,bshe->brhe",
        probs.astype(jnp.bfloat16),
        d_head_low,
        preferred_element_type=jnp.float32,
    )
    d_probs = jnp.einsum(
        "bshe,brhe->bhsr", d_head_low, value_rows, preferred_element_type=jnp.float32
    )
    d_scores = (probs * (d_probs - jnp.sum(probs * d_probs, axis=-1, keepdims=True))).astype(
        jnp.bfloat16
    )
    grad_q = (
        jnp.einsum("bhsr,brhe->bshe", d_scores, key_rows, preferred_element_type=jnp.float32)
        * score_scale
    )
    grad_k = (
        jnp.einsum("bhsr,bshe->brhe", d_scores, queries, preferred_element_type=jnp.float32)
        * score_scale
    )
    d_qkv_low = jnp.stack(
        [
            grad_q.reshape(row_count, local_width),
            grad_k.reshape(row_count, local_width),
            grad_v.reshape(row_count, local_width),
        ],
        axis=1,
    ).astype(jnp.bfloat16)
    grad_bias_qv = jnp.stack(
        [
            jnp.sum(d_qkv_low[:, 0], axis=0, dtype=jnp.float32),
            jnp.sum(d_qkv_low[:, 2], axis=0, dtype=jnp.float32),
        ]
    )
    grad_w_qkv = jnp.einsum(
        "td,tcf->dcf", normed_low, d_qkv_low, preferred_element_type=jnp.float32
    )
    d_normed_part = jnp.einsum("tcf,dcf->td", d_qkv_low, w_qkv, preferred_element_type=jnp.float32)
    d_normed = lax.psum(d_normed_part.astype(jnp.bfloat16), "tensor").astype(jnp.float32)
    d_input, grad_ln1_gain, grad_ln1_bias = first_pull(d_normed)
    token_grad = (d_input + d_resid) * row_mask
    sum_w_qkv, sum_w_proj, sum_w_fc1, sum_w_fc2 = (
        lax.psum_scatter(grad_w_qkv, "dp", scatter_dimension=0, tiled=True),
        lax.psum_scatter(grad_w_proj, "dp", scatter_dimension=1, tiled=True),
        lax.psum_scatter(grad_w_fc1, "dp", scatter_dimension=0, tiled=True),
        lax.psum_scatter(grad_w_fc2, "dp", scatter_dimension=1, tiled=True),
    )
    (
        sum_ln1_gain,
        sum_ln1_bias,
        sum_bias_qv,
        sum_bias_proj,
        sum_ln2_gain,
        sum_ln2_bias,
        sum_bias_fc1,
        sum_bias_fc2,
    ) = lax.psum(
        (
            grad_ln1_gain,
            grad_ln1_bias,
            grad_bias_qv,
            grad_bias_proj,
            grad_ln2_gain,
            grad_ln2_bias,
            grad_bias_fc1,
            grad_bias_fc2,
        ),
        "dp",
    )
    return (
        final_out.astype(jnp.bfloat16),
        loss_value,
        token_grad,
        sum_ln1_gain,
        sum_ln1_bias,
        sum_w_qkv,
        sum_bias_qv,
        sum_w_proj,
        sum_bias_proj,
        sum_ln2_gain,
        sum_ln2_bias,
        sum_w_fc1,
        sum_bias_fc1,
        sum_w_fc2,
        sum_bias_fc2,
    )


def solution(mesh):
    in_specs = (
        P("dp", None),
        P(),
        P("dp", None),
        P("dp", None),
        P(),
        P(),
        P(None, None, "tensor"),
        P(None, "tensor"),
        P("tensor", None),
        P(),
        P(),
        P(),
        P(None, "tensor"),
        P("tensor"),
        P("tensor", None),
        P(),
    )
    out_specs = (
        P("dp", None),
        P("dp"),
        P("dp", None),
        P(),
        P(),
        P("dp", None, "tensor"),
        P(None, "tensor"),
        P("tensor", "dp"),
        P(),
        P(),
        P(),
        P("dp", "tensor"),
        P("tensor"),
        P("tensor", "dp"),
        P(),
    )
    return jax.shard_map(body, mesh=mesh, in_specs=in_specs, out_specs=out_specs, check_vma=False)
```

profile of v0, /device:TPU:0, one launch (start us, length us, event | category | flops | bytes accessed | tf_op | source)
XLA Modules:
  0.0 677.0 jit_solution(13613605104122560235)
XLA Ops:
  10.3 2.2 fusion.16
  12.6 2.3 multiply_reduce_fusion.3
  15.1 2.5 add_convert_fusion.3
  19.8 2.4 copy.70
  23.5 2.4 copy.69
  25.9 2.7 reshape.177
  28.5 3.1 copy.71
  31.6 1.7 fusion.4
  33.3 1.6 exponential_reduce_fusion
  37.9 2.3 convert_element_type.147
  40.2 3.2 convolution_convert_fusion.2
  44.0 51.5 %all-reduce.6.cloned.1.call-done = bf16[960,1024]{1,0:T(8,128)(2,1)} async-done(((bf16[960,1024]{1,0:T(8,128)(2,1)}), bf16[960,1024]{1,0:T(8,128)(2,1)}) %all-reduce.6.cloned.1.call-update) | async-done | bytes 1966096 | tf_op jit(solution)/shard_map/psum | solution.py:87
  95.5 3.3 fusion.54
  100.2 13.3 %multiply_convert_fusion.1 = (bf16[960,1024]{1,0:T(8,128)(2,1)S(1)}, f32[960,1024]{1,0:T(8,128)}, f32[960,1024]{1,0:T(8,128)}) fusion(f32[1024]{0:T(1024)S(1)} %convert_element_type.154, bf16[1024,1024]{1,0:T(8,128)(2,1)S(1)} %copy-done, f32[1024]{0:T(1024)S(1)} %convert_element_type.152, f32[1024]{0:T(1024)S(1)} %convert_element_type.151, ...), kind=kOutput, calls=%fused_computation.33 | convolution fusion | flops 2087976960 | bytes 15887616 | tf_op jit(solution)/shard_map/dot_general | solution.py:93
  114.7 3.5 convolution_convert_fusion.1
  119.6 48.1 %all-reduce.8.cloned.1.call-done = bf16[960,1024]{1,0:T(8,128)(2,1)} async-done(((bf16[960,1024]{1,0:T(8,128)(2,1)}), bf16[960,1024]{1,0:T(8,128)(2,1)}) %all-reduce.8.cloned.1.call-update) | async-done | bytes 1966096 | tf_op jit(solution)/shard_map/psum | solution.py:99
  167.7 5.5 fusion.55
  173.4 1.8 copy-done.29
  175.1 3.8 convert_reduce_fusion.2
  180.2 3.5 convolution_convert_fusion
  183.8 49.4 %all-reduce.10.cloned.1.call-done = bf16[960,1024]{1,0:T(8,128)(2,1)} async-done(((bf16[960,1024]{1,0:T(8,128)(2,1)}), bf16[960,1024]{1,0:T(8,128)(2,1)}) %all-reduce.10.cloned.1.call-update) | async-done | bytes 1966096 | tf_op jit(solution)/shard_map/psum | solution.py:115
  233.3 4.9 convert_reduce_fusion.1
  238.3 7.3 %fusion.8 = (f32[1024]{0:T(1024)S(1)}, f32[960]{0:T(1024)S(1)}, f32[960]{0:T(1024)S(1)}, bf16[960,1024]{1,0:T(8,128)(2,1)}) fusion(bf16[960,1024]{1,0:T(8,128)(2,1)S(1)} %copy-done.10, f32[960]{0:T(1024)S(1)} %fusion.43, f32[960]{0:T(1024)S(1)} %broadcast_multiply_fusion, f32[1024]{0:T(1024)S(1)} %convert_element_type.150, ...), kind=kLoop, calls=%fused_computation.22 | loop fusion | flops 25556096 | bytes 11835904 | tf_op jit(solution)/shard_map/transpose(jvp())/reduce_sum | solution.py:19
  245.6 2.3 fusion.56
  247.9 1.9 copy-done.8
  251.3 2.7 reshape.180
  253.9 3.1 copy.75
  257.0 4.5 fusion.24
  261.5 5.0 multiply_reduce_fusion
  266.5 1.9 multiply_convert_fusion
  268.4 1.8 fusion.25
  272.3 1.8 stack_reshape.14
  279.1 3.1 copy.93
  282.2 2.7 reshape.176
  284.9 4.9 bitcast_convert_fusion
  289.8 4.0 fusion.27
  293.9 5.3 fusion.36
  299.2 7.2 %fusion.30 = f32[1024,1024]{1,0:T(8,128)} fusion(bf16[960,1024]{1,0:T(8,128)(2,1)} %copy-done.27, f32[960,1024]{1,0:T(8,128)} %copy-done.11), kind=kOutput, calls=%fused_computation.80 | convolution fusion | flops 2014248960 | bytes 10092544 | tf_op jit(solution)/shard_map/tf,te->fe/dot_general | solution.py:109
  306.7 7.0 %fusion.52 = f32[1024,1024]{1,0:T(8,128)} fusion(bf16[960,1024]{1,0:T(8,128)(2,1)} %copy-done.30, f32[1024]{0:T(1024)S(1)} %convert_element_type.152, f32[1024]{0:T(1024)S(1)} %convert_element_type.151, f32[960]{0:T(1024)S(1)} %fusion.43, f32[960]{0:T(1024)S(1)} %broadcast_multiply_fusion, bf16[960,1024]{1,0:T(8,128)(2,1)} %all-reduce.6.cloned.1.call-done, ...), kind=kOutput, calls=%fused_computation.112 | convolution fusion | flops 2023096320 | bytes 10116352 | tf_op jit(solution)/shard_map/td,tf->df/dot_general | solution.py:113
  315.5 23.8 %all-reduce.12.cloned.1.call-done = bf16[960,1024]{1,0:T(8,128)(2,1)} async-done(((bf16[960,1024]{1,0:T(8,128)(2,1)}), bf16[960,1024]{1,0:T(8,128)(2,1)}) %all-reduce.12.cloned.1.call-update) | async-done | bytes 1966096 | tf_op jit(solution)/shard_map/psum | solution.py:166
  339.3 3.1 convert_reduce_fusion
  342.4 2.8 fusion.9
  345.2 37.9 %all-reduce = (f32[1024]{0:T(1024)}, f32[1024]{0:T(1024)}, f32[2,256]{1,0:T(2,128)}, f32[1024]{0:T(1024)}, f32[1024]{0:T(1024)}, /*index=5*/f32[1024]{0:T(1024)}, f32[1024]{0:T(1024)}, f32[1024]{0:T(1024)}) all-reduce(f32[1024]{0:T(1024)S(1)} %get-tuple-element.17, ...), channel_id=1, replica_groups=mesh['dp'=8,'tensor'=4] {'dp'}, use_global_device_ids=true, to_apply=%region_19.20 | all-reduce | flops 7680 | bytes 61440 | tf_op jit(solution)/shard_map/psum | solution.py:184
  383.1 5.5 add_multiply_fusion
  388.6 18.6 %reduce-scatter.7.cloned.1.call-done = f32[256,128]{1,0:T(8,128)} async-done(((f32[256,1024]{1,0:T(8,128)}), f32[256,128]{1,0:T(8,128)}) %reduce-scatter.7.cloned.1.call-update) | async-done | bytes 131088 | tf_op jit(solution)/shard_map/reduce_scatter | solution.py:171
  407.2 78.6 %reduce-scatter.5.cloned.1.call-done = f32[128,3,256]{2,0,1:T(8,128)} async-done(((f32[1024,3,256]{2,0,1:T(8,128)}), f32[128,3,256]{2,0,1:T(8,128)}) %reduce-scatter.5.cloned.1.call-update) | async-done | bytes 393232 | tf_op jit(solution)/shard_map/reduce_scatter | solution.py:170
  485.8 92.1 %reduce-scatter.11.cloned.1.call-done = f32[1024,128]{1,0:T(8,128)} async-done(((f32[1024,1024]{1,0:T(8,128)}), f32[1024,128]{1,0:T(8,128)}) %reduce-scatter.11.cloned.1.call-update) | async-done | bytes 524304 | tf_op jit(solution)/shard_map/reduce_scatter | solution.py:173
  577.9 91.9 %reduce-scatter.9.cloned.1.call-done = f32[128,1024]{1,0:T(8,128)} async-done(((f32[1024,1024]{1,0:T(8,128)}), f32[128,1024]{1,0:T(8,128)}) %reduce-scatter.9.cloned.1.call-update) | async-done | bytes 524304 | tf_op jit(solution)/shard_map/reduce_scatter | solution.py:172
  (123 shorter events, 25.2 us)
Async XLA Ops:
  7.2 93.0 %copy-start = (bf16[1024,1024]{1,0:T(8,128)(2,1)S(1)}, bf16[1024,1024]{1,0:T(8,128)(2,1)}, u32[]{:S(2)}) copy-start(bf16[1024,1024]{1,0:T(8,128)(2,1)} %param.28) | copy-start | bytes 6291460
  7.2 88.3 %all-reduce.6.cloned.1.call-start = ((), (), s32[]{:S(2)}) async-start(), calls=%async_computation.4 | async-start | bytes 3932160 | tf_op jit(solution)/shard_map/psum | solution.py:87
  10.3 4.7 copy-start.2
  10.3 4.7 copy-start.25
  33.3 3.2 copy-start.5
  33.3 1.7 copy-start.14
  36.5 7.4 %copy-start.18 = (bf16[1024]{0:T(1024)(128)(2,1)S(1)}, bf16[1024]{0:T(1024)(128)(2,1)}, u32[]{:S(2)}) copy-start(bf16[1024]{0:T(1024)(128)(2,1)} %param.25) | copy-start | bytes 6148
  36.5 7.5 %copy-start.19 = (bf16[1024]{0:T(1024)(128)(2,1)S(1)}, bf16[1024]{0:T(1024)(128)(2,1)}, u32[]{:S(2)}) copy-start(bf16[1024]{0:T(1024)(128)(2,1)} %param.26) | copy-start | bytes 6148
  36.5 7.5 %copy-start.20 = (bf16[1024]{0:T(1024)(128)(2,1)S(1)}, bf16[1024]{0:T(1024)(128)(2,1)}, u32[]{:S(2)}) copy-start(bf16[1024]{0:T(1024)(128)(2,1)} %param.27) | copy-start | bytes 6148
  36.5 7.5 %copy-start.21 = (bf16[1024]{0:T(1024)(128)(2,1)S(1)}, bf16[1024]{0:T(1024)(128)(2,1)}, u32[]{:S(2)}) copy-start(bf16[1024]{0:T(1024)(128)(2,1)} %param.29) | copy-start | bytes 6148
  43.4 124.3 %all-reduce.8.cloned.1.call-start = ((), (), s32[]{:S(2)}) async-start(), calls=%async_computation.5 | async-start | bytes 3932160 | tf_op jit(solution)/shard_map/psum | solution.py:99
  95.5 3.3 copy-start.3
  95.5 3.3 copy-start.6
  100.1 14.6 %copy-start.23 = (bf16[1024,1024]{1,0:T(8,128)(2,1)S(1)}, bf16[1024,1024]{1,0:T(8,128)(2,1)}, u32[]{:S(2)}) copy-start(bf16[1024,1024]{1,0:T(8,128)(2,1)} %param.30) | copy-start | bytes 6291460
  113.4 1.3 copy-start.27
  114.7 3.6 copy-start.22
  114.7 3.6 copy-start.26
  118.2 115.0 %all-reduce.10.cloned.1.call-start = ((), (), s32[]{:S(2)}) async-start(), calls=%async_computation.6 | async-start | bytes 3932160 | tf_op jit(solution)/shard_map/psum | solution.py:115
  167.7 5.5 copy-start.24
  167.7 5.6 copy-start.28
  167.7 7.4 %copy-start.29 = (f32[960,1024]{1,0:T(8,128)S(1)}, f32[960,1024]{1,0:T(8,128)}, u32[]{:S(2)}) copy-start(f32[960,1024]{1,0:T(8,128)} %get-tuple-element.48) | copy-start | bytes 11796484
  173.2 5.7 copy-start.11
  178.9 1.3 copy-start.30
  183.8 54.4 %copy-start.4 = (bf16[960,1024]{1,0:T(8,128)(2,1)S(1)}, bf16[960,1024]{1,0:T(8,128)(2,1)}, u32[]{:S(2)}) copy-start(bf16[960,1024]{1,0:T(8,128)(2,1)} %param.16) | copy-start | bytes 5898244
  183.8 155.5 %all-reduce.12.cloned.1.call-start = ((), (), s32[]{:S(2)}) async-start(), calls=%async_computation.7 | async-start | bytes 3932160 | tf_op jit(solution)/shard_map/psum | solution.py:166
  233.3 4.9 copy-start.7
  233.3 4.9 copy-start.10
  233.3 4.9 copy-start.13
  238.3 7.3 %copy-start.12 = (f32[960,1024]{1,0:T(8,128)S(1)}, f32[960,1024]{1,0:T(8,128)}, u32[]{:S(2)}) copy-start(f32[960,1024]{1,0:T(8,128)} %copy-done.11) | copy-start | bytes 11796484
  245.6 4.2 copy-start.17
  247.8 1.9 copy-start.8
  257.0 4.5 copy-start.15
  257.0 4.5 copy-start.16
  257.0 9.5 %slice-start = ((s8[5898240]{0:T(1024)(128)(4,1)}), s8[4194304]{0:T(1024)(128)(4,1)S(1)}, s32[]{:S(2)}) async-start(s8[5898240]{0:T(1024)(128)(4,1)} %bitcast.53), calls=%async_computation.12 | async-start | bytes 8388608
  261.5 5.0 slice-start.1
  289.8 117.5 %reduce-scatter.7.cloned.1.call-start = ((), (), s32[]{:S(2)}) async-start(), calls=%async_computation.9 | async-start | bytes 1179648 | tf_op jit(solution)/shard_map/reduce_scatter | solution.py:171
  293.8 192.0 %reduce-scatter.5.cloned.1.call-start = ((), (), s32[]{:S(2)}) async-start(), calls=%async_computation.8 | async-start | bytes 3538944 | tf_op jit(solution)/shard_map/reduce_scatter | solution.py:170
  299.2 278.7 %reduce-scatter.11.cloned.1.call-start = ((), (), s32[]{:S(2)}) async-start(), calls=%async_computation.11 | async-start | bytes 4718592 | tf_op jit(solution)/shard_map/reduce_scatter | solution.py:173
  306.4 363.3 %reduce-scatter.9.cloned.1.call-start = ((), (), s32[]{:S(2)}) async-start(), calls=%async_computation.10 | async-start | bytes 4718592 | tf_op jit(solution)/shard_map/reduce_scatter | solution.py:172
  339.3 3.1 copy-start.9
  383.1 286.6 %copy-start.1 = (bf16[1024,1024]{1,0:T(8,128)(2,1)S(1)}, bf16[1024,1024]{1,0:T(8,128)(2,1)}, u32[]{:S(2)}) copy-start(bf16[1024,1024]{1,0:T(8,128)(2,1)} %param.28) | copy-start | bytes 6291460
Sparse Core Ops, SparseCore 0:
  43.5 51.9 all-reduce.5
  118.4 49.3 all-reduce.7
  183.9 49.3 all-reduce.9
  289.9 49.3 all-reduce.11
  343.1 64.0 reduce-scatter.6
  411.7 74.0 reduce-scatter.4
  490.4 87.3 reduce-scatter.10
  582.1 87.6 reduce-scatter.8
where the time goes:
time: 685 us; the launch traced here: 677 us
  waiting for transfers between devices  454 us (66%)
  matrix products  74.7 us (11%)
  other arithmetic  47.9 us (7%)
  local copies, waits for them, and re-layouts  44.9 us (7%)
  blocking collectives  37.9 us (6%)
  between operations  16.5 us (2%)
    reduce_scatter x1, waiting for transfers between devices, body(): lax.psum_scatter(grad_w_fc2, 'dp', scatter_dimension=1, tiled=True)  92.1 us
    reduce_scatter x1, waiting for transfers between devices, body(): lax.psum_scatter(grad_w_fc1, 'dp', scatter_dimension=0, tiled=True)  91.9 us
    reduce_scatter x1, waiting for transfers between devices, body(): lax.psum_scatter(grad_w_qkv, 'dp', scatter_dimension=0, tiled=True)  78.6 us
    psum x1, waiting for transfers between devices, body(): lax.psum(attn_part.astype(jnp.bfloat16), 'tensor').astype(jnp.float32)  51.5 us
    psum x1, waiting for transfers between devices, body(): lax.psum(d_second_part.astype(jnp.bfloat16), 'tensor').astype(jnp.float32)  49.4 us
    psum x1, waiting for transfers between devices, body(): lax.psum(mlp_part.astype(jnp.bfloat16), 'tensor').astype(jnp.float32)  48.1 us
    psum x1, blocking collectives, body(): lax.psum((grad_ln1_gain, grad_ln1_bias, grad_bias_qv, grad_bias_proj, gra...  37.9 us
    psum x1, waiting for transfers between devices, body(): lax.psum(d_normed_part.astype(jnp.bfloat16), 'tensor').astype(jnp.float32)  23.8 us
  transfers between devices with their start and end apart: 8, of which 8 were waited for; matrix products, arithmetic and copies ran while one was open for 5% of the time, Pallas kernels for 0%

commit v1 on v0

v1 whole, which is shorter than its diff:
```python
import functools

import jax
import jax.numpy as jnp
from jax import lax
from jax.experimental import pallas as pl
from jax.experimental.pallas import tpu as pltpu
from jax.sharding import PartitionSpec as P

D = 1024
H = 16
HEAD = D // H
BUFFER = 64
SLOTS = 320
HALF = D // 2
RB = 32
EPS = 1e-06
F32 = jnp.float32
BF16 = jnp.bfloat16
MESH = pl.DeviceIdType.MESH
NT = (((1,), (1,)), ((), ()))
TN = (((0,), (0,)), ((), ()))
NN = (((1,), (0,)), ((), ()))
INV_SQRT2 = 0.7071067811865476
INV_SQRT_2PI = 0.3989422804014327


def mm(a, b, dims):
    return lax.dot_general(a, b, dims, preferred_element_type=F32)


def fold8(x):
    return jnp.sum(x.reshape(x.shape[0] // 8, 8, x.shape[1]), axis=0)


def kernel(
    cfg,
    kept_ref, vec_ref, tok_in, tea_in, og_in, wqkv_in, wproj_in, wfc1_in, wfc2_in,
    out_hbm, tg_hbm, loss_ref, vout_ref, gfc2_ref, gfc1_ref, gproj_ref, gqkv_ref,
    wqkv, wproj, wfc1, wfc2, tok, tea, og,
    a_r, qkv_r, heads_r, c_r, h1_r, act_r, gp_r, seed_r, sl_r, dpre_r, dqkv_r,
    core_s, core_r, tot, gs, yr, zr, lacc, vacc, vs, vyr, vzr,
    in_sem, out_sem, ps_s, ps_r, y_s, y_r, z_s, z_r, v_s, v_r,
):
    S, NZ, CH, MB, NBLK, NZB, FW = cfg
    LW = wproj.shape[0]
    R = SLOTS
    rows_all = S * R
    dp = lax.axis_index("dp")
    t = lax.axis_index("tensor")
    y = lax.rem(dp, 2)
    z = dp // 2
    lo = lax.rem(t, 2)
    hi = t // 2
    sib = (dp, hi * 2 + (1 - lo))
    xn = (dp, (1 - hi) * 2 + lo)
    yn = (z * 2 + (1 - y), t)

    def zn(zz):
        return (zz * 2 + y, t)

    def in_copy(i, src, dst):
        return pltpu.make_async_copy(src, dst, in_sem.at[i])

    ins = [
        in_copy(0, tok_in, tok),
        in_copy(1, wqkv_in, wqkv),
        in_copy(2, wproj_in, wproj),
        in_copy(3, wfc1_in, wfc1),
        in_copy(4, wfc2_in, wfc2),
        in_copy(5, tea_in, tea),
        in_copy(6, og_in, og),
    ]
    for c in ins:
        c.start()

    bar = pltpu.get_barrier_semaphore()
    for peer in (sib, xn, yn):
        pl.semaphore_signal(bar, inc=1, device_id=peer, device_id_type=MESH)

    def bar_z(k, _):
        pl.semaphore_signal(bar, inc=1, device_id=zn(lax.rem(z + k, NZ)), device_id_type=MESH)
        return 0

    lax.fori_loop(1, NZ, bar_z, 0)
    pl.semaphore_wait(bar, 3 + NZ - 1)

    vacc[...] = jnp.zeros_like(vacc)
    count = lax.fori_loop(
        0, kept_ref.shape[0], lambda i, acc: acc + (kept_ref[i] + BUFFER).astype(F32), jnp.float32(0.0)
    )

    def length(s):
        return kept_ref[dp * S + s] + BUFFER

    def mask_rows(s, i):
        idx = lax.broadcasted_iota(jnp.int32, (RB, 1), 0) + i * RB
        return (idx < length(s)).astype(F32)

    def seq_rows(s):
        return pl.ds(pl.multiple_of(s * R, 64), R)

    def chunks(fn, init=0):
        return lax.fori_loop(0, R // RB, fn, init)

    def blk(s, i):
        return pl.ds(pl.multiple_of(s * R + i * RB, RB), RB)

    def loc(i):
        return pl.ds(pl.multiple_of(i * RB, RB), RB)

    def norm_stats(x):
        mean = jnp.mean(x, axis=-1, keepdims=True)
        off = x - mean
        var = jnp.mean(off * off, axis=-1, keepdims=True)
        r = lax.rsqrt(var + EPS)
        return off * r, r

    def cp(p, s, kind, src, dst, dev):
        return pltpu.make_async_remote_copy(
            src_ref=src, dst_ref=dst,
            send_sem=ps_s.at[p, s, kind], recv_sem=ps_r.at[p, s, kind],
            device_id=dev, device_id_type=MESH,
        )

    def cp_core(p, s):
        return cp(p, s, 0, core_s.at[s], core_r.at[s], sib)

    def cp_x(p, s):
        ref = tot.at[p, s, lo, hi]
        return cp(p, s, 1, ref, ref, xn)

    def cp_f1(p, s):
        ref = tot.at[p, s, lo, hi]
        return cp(p, s, 2, ref, ref, sib)

    def cp_f2(p, s):
        ref = tot.at[p, s, lo, 1 - hi]
        return cp(p, s, 3, ref, ref, sib)

    def ps_start(p, s, part):
        core_s[s] = part(1 - lo).astype(BF16)
        cp_core(p, s).start()
        own = part(lo).astype(BF16).astype(F32)
        cp_core(p, s).wait_recv()
        tot[p, s, lo, hi] = (own + core_r[s].astype(F32)).astype(BF16)
        cp_x(p, s).start()
        cp_f1(p, s).start()

    def ps_finish(p, s):
        cp_core(p, s).wait_send()
        cp_x(p, s).wait()
        cp_f2(p, s).start()
        cp_f1(p, s).wait()
        cp_f2(p, s).wait()

    def ps_total(p, s, i):
        rr = loc(i)
        parts = [
            tot[p, s, h, 0, rr, :].astype(F32) + tot[p, s, h, 1, rr, :].astype(F32) for h in range(2)
        ]
        return jnp.concatenate(parts, axis=1)

    def half_cols(h):
        return pl.ds(pl.multiple_of(h * HALF, HALF), HALF)

    lane_half = lax.broadcasted_iota(jnp.int32, (1, 2 * HEAD), 1) // HEAD

    def head_mask(hh):
        return (lane_half == hh).astype(F32).astype(BF16)

    def pair_cols(c, hp):
        return pl.ds(pl.multiple_of(c * LW + hp * 2 * HEAD, 2 * HEAD), 2 * HEAD)

    def probs_of(qm, k, s):
        sc = mm(qm, k, NT) * (HEAD ** -0.5)
        col = lax.broadcasted_iota(jnp.int32, (1, R), 1)
        sc = jnp.where(col < length(s), sc, -1e30)
        top = jnp.max(sc, axis=-1, keepdims=True)
        e = jnp.exp(sc - top)
        return e / jnp.sum(e, axis=-1, keepdims=True)

    npair = LW // (2 * HEAD)

    ins[0].wait()
    ins[1].wait()
    ins[2].wait()

    def phase_a(s, _):
        def ln(i, _):
            x = tok[blk(s, i), :].astype(F32) * mask_rows(s, i)
            hat, _r = norm_stats(x)
            a_r[blk(s, i), :] = (hat * vec_ref[0:1, :] + vec_ref[1:2, :]).astype(BF16)
            return 0

        chunks(ln)
        rs = seq_rows(s)
        av = a_r[rs, :]
        for c in range(3):
            cs = slice(c * LW, (c + 1) * LW)
            qkv_r[rs, cs] = (mm(av, wqkv[:, cs], NN) + vec_ref[7:8, cs]).astype(BF16)

        def pair(hp, _):
            q = qkv_r[rs, pair_cols(0, hp)]
            k = qkv_r[rs, pair_cols(1, hp)]
            v = qkv_r[rs, pair_cols(2, hp)]
            o = None
            for hh in range(2):
                pr = probs_of(q * head_mask(hh), k, s).astype(BF16)
                oh = mm(pr, v * head_mask(hh), NN)
                o = oh if o is None else o + oh
            heads_r[rs, pair_cols(0, hp)] = o.astype(BF16)
            return 0

        lax.fori_loop(0, npair, pair, 0)
        hv = heads_r[rs, :]
        ps_start(0, s, lambda h: mm(hv, wproj[:, half_cols(h)], NN))
        return 0

    lax.fori_loop(0, S, phase_a, 0)

    ins[3].wait()
    ins[4].wait()

    def phase_b(s, _):
        ps_finish(0, s)

        def ln(i, _):
            x = tok[blk(s, i), :].astype(F32) * mask_rows(s, i)
            h1 = x + ps_total(0, s, i) + vec_ref[2:3, :]
            h1_r[blk(s, i), :] = h1
            hat, _r = norm_stats(h1)
            c_r[blk(s, i), :] = (hat * vec_ref[3:4, :] + vec_ref[4:5, :]).astype(BF16)
            return 0

        chunks(ln)
        rs = seq_rows(s)
        cv = c_r[rs, :]

        def fc1(j, _):
            cs = pl.ds(pl.multiple_of(j * 256, 256), 256)
            pre = mm(cv, wfc1[:, cs], NN) + vec_ref[5:6, cs]
            phi = 0.5 * (1.0 + lax.erf(pre * INV_SQRT2))
            act_r[rs, cs] = (pre * phi).astype(BF16)
            gp_r[rs, cs] = phi + pre * (INV_SQRT_2PI * jnp.exp(-0.5 * pre * pre))
            return 0

        lax.fori_loop(0, FW // 256, fc1, 0)
        ps_start(1, s, lambda h: mm(act_r[rs, :], wfc2[:, half_cols(h)], NN))
        return 0

    lax.fori_loop(0, S, phase_b, 0)

    ins[5].wait()
    ins[6].wait()
    loss_scale = kept_ref.shape[0] / (2.0 * count * D)
    seed_scale = kept_ref.shape[0] * SLOTS * 1.0 / count

    def out_copy(s):
        return pltpu.make_async_copy(tea.at[seq_rows(s), :], out_hbm.at[seq_rows(s), :], out_sem.at[0, s])

    def tg_copy(s):
        return pltpu.make_async_copy(seed_r.at[seq_rows(s), :], tg_hbm.at[seq_rows(s), :], out_sem.at[1, s])

    def phase_c(s, _):
        ps_finish(1, s)
        lacc[...] = jnp.zeros_like(lacc)

        def fin(i, _):
            m = mask_rows(s, i)
            final = (h1_r[blk(s, i), :] + ps_total(1, s, i) + vec_ref[6:7, :]) * m
            diff = (final - tea[blk(s, i), :].astype(F32)) * m
            seed = (og[blk(s, i), :].astype(F32) + diff * seed_scale) * m
            tea[blk(s, i), :] = final.astype(BF16)
            seed_r[blk(s, i), :] = seed
            sl_r[blk(s, i), :] = seed.astype(BF16)
            lacc[...] += fold8(diff * diff)
            vacc[6] += fold8(seed)
            return 0

        chunks(fin)
        out_copy(s).start()
        loss_ref[s] = jnp.sum(lacc[...]) * loss_scale
        rs = seq_rows(s)
        sv = sl_r[rs, :]

        def dact(j, _):
            cs = pl.ds(pl.multiple_of(j * 256, 256), 256)
            d = mm(sv, wfc2[cs, :], NT) * gp_r[rs, cs]
            dl = d.astype(BF16)
            dpre_r[rs, cs] = dl
            vacc[5, :, cs] += fold8(dl.astype(F32))
            return 0

        lax.fori_loop(0, FW // 256, dact, 0)
        ps_start(0, s, lambda h: mm(dpre_r[rs, :], wfc1[half_cols(h), :], NT))
        return 0

    lax.fori_loop(0, S, phase_c, 0)

    def block_at(k):
        return lax.rem(z // NZB + 1 + k, NBLK)

    def cp_y(tile):
        return pltpu.make_async_remote_copy(
            src_ref=gs.at[tile, :, 1 - y], dst_ref=yr.at[tile],
            send_sem=y_s.at[tile], recv_sem=y_r.at[tile], device_id=yn, device_id_type=MESH,
        )

    def cp_z(g, tile, i, zz):
        slot = lax.rem(zz - z + NZ, NZ) - 1
        return pltpu.make_async_remote_copy(
            src_ref=yr.at[tile, i], dst_ref=zr.at[g, slot],
            send_sem=z_s.at[tile, i], recv_sem=z_r.at[g, slot], device_id=zn(zz), device_id_type=MESH,
        )

    def grad_tiles(g, lhs, parts):
        def one(k, _):
            cols = pl.ds(pl.multiple_of(block_at(k) * MB, MB), MB)
            tile = g * NBLK + k
            off = 0
            for lref, rref in parts:
                n = rref.shape[1]
                val = mm(lref[:, cols], rref[...], TN)
                gs[tile, :, :, :, off:off + n] = val.astype(BF16).reshape(NZB, 2, CH, n)
                off += n
            cp_y(tile).start()
            return 0

        lax.fori_loop(0, NBLK, one, 0)

    def z_stage(g, k):
        tile = g * NBLK + k
        cp_y(tile).wait_recv()

        def one(i, _):
            zz = block_at(k) * NZB + i
            yr[tile, i] = (gs[tile, i, y].astype(F32) + yr[tile, i].astype(F32)).astype(BF16)

            @pl.when(zz != z)
            def _():
                cp_z(g, tile, i, zz).start()

            return 0

        lax.fori_loop(0, NZB, one, 0)

    def z_stages(g):
        def one(k, _):
            z_stage(g, k)
            return 0

        lax.fori_loop(0, NBLK, one, 0)

    def grad_final(g, outs):
        def wait(j, _):
            zz = lax.rem(z + 1 + j, NZ)
            pltpu.make_async_remote_copy(
                src_ref=yr.at[0, 0], dst_ref=zr.at[g, j], send_sem=z_s.at[0, 0],
                recv_sem=z_r.at[g, j], device_id=zn(zz), device_id_type=MESH,
            ).wait_recv()
            return 0

        lax.fori_loop(0, NZ - 1, wait, 0)
        own_tile = g * NBLK + NBLK - 1
        own_i = lax.rem(z, NZB)
        off = 0
        for ref in outs:
            n = ref.shape[1]
            ref[...] = yr[own_tile, own_i, :, off:off + n].astype(F32)

            def add(j, _):
                ref[...] += zr[g, j, :, off:off + n].astype(F32)
                return 0

            lax.fori_loop(0, NZ - 1, add, 0)
            off += n

    grad_tiles(0, sl_r, [(sl_r, act_r)])
    grad_tiles(1, c_r, [(c_r, dpre_r)])

    def phase_d(s, _):
        ps_finish(0, s)

        def lnb(i, _):
            hat, r = norm_stats(h1_r[blk(s, i), :])
            dy = ps_total(0, s, i)
            vacc[3] += fold8(dy * hat)
            vacc[4] += fold8(dy)
            dg = dy * vec_ref[3:4, :]
            m1 = jnp.mean(dg, axis=-1, keepdims=True)
            m2 = jnp.mean(dg * hat, axis=-1, keepdims=True)
            dh1 = seed_r[blk(s, i), :] + r * (dg - m1 - hat * m2)
            seed_r[blk(s, i), :] = dh1
            vacc[2] += fold8(dh1)
            sl_r[blk(s, i), :] = dh1.astype(BF16)
            return 0

        chunks(lnb)
        rs = seq_rows(s)

        def pair(hp, _):
            wc = pl.ds(pl.multiple_of(hp * 2 * HEAD, 2 * HEAD), 2 * HEAD)
            dh = mm(sl_r[rs, :], wproj[wc, :], NT).astype(BF16)
            q = qkv_r[rs, pair_cols(0, hp)]
            k = qkv_r[rs, pair_cols(1, hp)]
            v = qkv_r[rs, pair_cols(2, hp)]
            dq = dk = dv = None
            for hh in range(2):
                hm = head_mask(hh)
                qm, km, dm = q * hm, k * hm, dh * hm
                pr = probs_of(qm, k, s)
                dpr = mm(dm, v, NT)
                ds = (pr * (dpr - jnp.sum(pr * dpr, axis=-1, keepdims=True))).astype(BF16)
                q1, k1, v1 = mm(ds, km, NN), mm(ds, qm, TN), mm(pr.astype(BF16), dm, TN)
                if dq is None:
                    dq, dk, dv = q1, k1, v1
                else:
                    dq, dk, dv = dq + q1, dk + k1, dv + v1
            dql = (dq * (HEAD ** -0.5)).astype(BF16)
            dvl = dv.astype(BF16)
            dqkv_r[rs, pair_cols(0, hp)] = dql
            dqkv_r[rs, pair_cols(1, hp)] = (dk * (HEAD ** -0.5)).astype(BF16)
            dqkv_r[rs, pair_cols(2, hp)] = dvl
            vacc[7, :, pair_cols(0, hp)] += fold8(dql.astype(F32))
            vacc[7, :, pair_cols(1, hp)] += fold8(dvl.astype(F32))
            return 0

        lax.fori_loop(0, npair, pair, 0)
        ps_start(1, s, lambda h: mm(dqkv_r[rs, :], wqkv[half_cols(h), :], NT))
        return 0

    lax.fori_loop(0, S, phase_d, 0)
    grad_tiles(2, None, [(sl_r, heads_r), (a_r, dqkv_r)])
    z_stages(0)

    def phase_e(s, _):
        ps_finish(1, s)

        def lnb(i, _):
            m = mask_rows(s, i)
            hat, r = norm_stats(tok[blk(s, i), :].astype(F32) * m)
            dy = ps_total(1, s, i)
            vacc[0] += fold8(dy * hat)
            vacc[1] += fold8(dy)
            dg = dy * vec_ref[0:1, :]
            m1 = jnp.mean(dg, axis=-1, keepdims=True)
            m2 = jnp.mean(dg * hat, axis=-1, keepdims=True)
            seed_r[blk(s, i), :] = (seed_r[blk(s, i), :] + r * (dg - m1 - hat * m2)) * m
            return 0

        chunks(lnb)
        tg_copy(s).start()
        return 0

    lax.fori_loop(0, S, phase_e, 0)

    for j in range(8):
        vs[j:j + 1, :] = jnp.sum(vacc[j], axis=0, keepdims=True)
    vy = pltpu.make_async_remote_copy(
        src_ref=vs, dst_ref=vyr, send_sem=v_s.at[0], recv_sem=v_r.at[0], device_id=yn, device_id_type=MESH
    )
    vy.start()

    z_stages(1)
    vy.wait()
    vzr[z] = vs[...] + vyr[...]

    def cp_v(k, zz):
        return pltpu.make_async_remote_copy(
            src_ref=vzr.at[z], dst_ref=vzr.at[z], send_sem=v_s.at[k], recv_sem=v_r.at[k],
            device_id=zn(zz), device_id_type=MESH,
        )

    def v_go(k, _):
        cp_v(k, lax.rem(z + k, NZ)).start()
        return 0

    lax.fori_loop(1, NZ, v_go, 0)
    z_stages(2)

    def v_wait(k, _):
        src = lax.rem(z - k + NZ, NZ)
        c = pltpu.make_async_remote_copy(
            src_ref=vzr.at[z], dst_ref=vzr.at[src], send_sem=v_s.at[k], recv_sem=v_r.at[k],
            device_id=zn(lax.rem(z + k, NZ)), device_id_type=MESH,
        )
        c.wait_recv()
        cp_v(k, lax.rem(z + k, NZ)).wait_send()
        return 0

    lax.fori_loop(1, NZ, v_wait, 0)
    vout_ref[...] = jnp.zeros_like(vout_ref)

    def v_add(k, _):
        vout_ref[...] += vzr[k]
        return 0

    lax.fori_loop(0, NZ, v_add, 0)

    grad_final(0, [gfc2_ref])
    grad_final(1, [gfc1_ref])
    grad_final(2, [gproj_ref, gqkv_ref])

    def drain_y(tile, _):
        cp_y(tile).wait_send()
        return 0

    lax.fori_loop(0, 3 * NBLK, drain_y, 0)
    for g in range(3):
        def drain_z(k, _):
            def one(i, _):
                zz = block_at(k) * NZB + i

                @pl.when(zz != z)
                def _():
                    cp_z(g, g * NBLK + k, i, zz).wait_send()

                return 0

            lax.fori_loop(0, NZB, one, 0)
            return 0

        lax.fori_loop(0, NBLK, drain_z, 0)

    def drain_out(s, _):
        out_copy(s).wait()
        tg_copy(s).wait()
        return 0

    lax.fori_loop(0, S, drain_out, 0)


def body(
    n_dp,
    tokens, kept, teacher, out_grad, ln1_gain, ln1_bias, w_qkv, bias_qv, w_proj, bias_proj,
    ln2_gain, ln2_bias, w_fc1, bias_fc1, w_fc2, bias_fc2,
):
    rows = tokens.shape[0]
    S = rows // SLOTS
    LW = w_qkv.shape[2]
    FW = w_fc1.shape[1]
    NZ = n_dp // 2
    CH = D // n_dp
    MB = max(256, 2 * CH)
    NBLK = D // MB
    NZB = MB // (2 * CH)
    T = 3 * NBLK
    cfg = (S, NZ, CH, MB, NBLK, NZB, FW)
    qb = jnp.concatenate([bias_qv[0], jnp.zeros_like(bias_qv[0]), bias_qv[1], jnp.zeros((D - 3 * LW,), BF16)])
    vec = jnp.stack(
        [ln1_gain, ln1_bias, bias_proj, ln2_gain, ln2_bias, bias_fc1, bias_fc2, qb]
    ).astype(F32)
    any_spec = pl.BlockSpec(memory_space=pl.ANY)
    vm = pl.BlockSpec(memory_space=pltpu.VMEM)
    sm = pl.BlockSpec(memory_space=pltpu.SMEM)
    sds = jax.ShapeDtypeStruct
    DMA = pltpu.SemaphoreType.DMA
    V = pltpu.VMEM
    out, token_grad, loss, vout, gfc2, gfc1, gproj, gqkv = pl.pallas_call(
        functools.partial(kernel, cfg),
        out_shape=[
            sds((rows, D), BF16), sds((rows, D), F32), sds((S,), F32), sds((8, D), F32),
            sds((CH, FW), F32), sds((CH, FW), F32), sds((CH, LW), F32), sds((CH, 3 * LW), F32),
        ],
        in_specs=[sm, vm] + [any_spec] * 7,
        out_specs=[any_spec, any_spec, sm] + [vm] * 5,
        scratch_shapes=[
            V((D, 3 * LW), BF16), V((LW, D), BF16), V((D, FW), BF16), V((FW, D), BF16),
            V((rows, D), BF16), V((rows, D), BF16), V((rows, D), BF16),
            V((rows, D), BF16), V((rows, 3 * LW), BF16), V((rows, LW), BF16), V((rows, D), BF16),
            V((rows, D), F32), V((rows, FW), BF16), V((rows, FW), F32), V((rows, D), F32),
            V((rows, D), BF16), V((rows, FW), BF16), V((rows, 3 * LW), BF16),
            V((S, SLOTS, HALF), BF16), V((S, SLOTS, HALF), BF16), V((2, S, 2, 2, SLOTS, HALF), BF16),
            V((T, NZB, 2, CH, 1024), BF16), V((T, NZB, CH, 1024), BF16), V((3, NZ - 1, CH, 1024), BF16),
            V((8, D), F32), V((8, 8, D), F32), V((8, D), F32), V((8, D), F32), V((NZ, 8, D), F32),
            DMA((7,)), DMA((2, S)), DMA((2, S, 4)), DMA((2, S, 4)), DMA((T,)), DMA((T,)),
            DMA((T, NZB)), DMA((3, NZ - 1)), DMA((NZ,)), DMA((NZ,)),
        ],
        compiler_params=pltpu.CompilerParams(
            collective_id=0, has_side_effects=True, vmem_limit_bytes=64 * 2**20 - 2**18
        ),
        name="layer",
    )(
        kept, vec, tokens, teacher, out_grad, w_qkv.reshape(D, 3 * LW), w_proj, w_fc1, w_fc2,
    )
    return (
        out, loss, token_grad, vout[0], vout[1], gqkv.reshape(CH, 3, LW),
        jnp.stack([vout[7, :LW], vout[7, LW:2 * LW]]), gproj.T, vout[2], vout[3], vout[4],
        gfc1, vout[5], gfc2.T, vout[6],
    )


def solution(mesh):
    tp = P("tensor")
    in_specs = (
        P("dp", None), P(), P("dp", None), P("dp", None), P(), P(), P(None, None, "tensor"),
        P(None, "tensor"), P("tensor", None), P(), P(), P(), P(None, "tensor"), tp, P("tensor", None), P(),
    )
    out_specs = (
        P("dp", None), P("dp"), P("dp", None), P(), P(), P("dp", None, "tensor"), P(None, "tensor"),
        P("tensor", "dp"), P(), P(), P(), P("dp", "tensor"), tp, P("tensor", "dp"), P(),
    )
    return jax.shard_map(
        functools.partial(body, mesh.shape["dp"]), mesh=mesh, in_specs=in_specs, out_specs=out_specs,
        check_vma=False,
    )
```

time: 685 us -> 203 us (0.30)
  waiting for transfers between devices: 454 us -> 0 us
  Pallas kernels: 0 us -> 175 us
  matrix products: 74.7 us -> 0 us
  other arithmetic: 47.9 us -> 1.22 us
  blocking collectives: 37.9 us -> 0 us
  local copies, waits for them, and re-layouts: 44.9 us -> 22.9 us
  between operations: 16.5 us -> 0.71 us
    reduce_scatter x4 -> x0, waiting for transfers between devices: 281 us -> none  [the longest x1 92.1 us: body(): lax.psum_scatter(grad_w_fc2, 'dp', scatter_dimension=1, tiled=True)]
    pallas_call x0 -> x1, Pallas kernels: none -> 175 us  [body(): pl.pallas_call(functools.partial(kernel, cfg), out_shape=[sds((rows, D),...]
    psum x4 -> x0, waiting for transfers between devices: 173 us -> none  [the longest x1 51.5 us: body(): lax.psum(attn_part.astype(jnp.bfloat16), 'tensor').astype(jnp.float32)]
    dot_general x18 -> x0, matrix products: 74.7 us -> none  [the longest x1 13.3 us: body(): jnp.dot(second_low, w_fc1, preferred_element_type=jnp.float32)]
    psum x1 -> x0, blocking collectives: 37.9 us -> none  [body(): lax.psum((grad_ln1_gain, grad_ln1_bias, grad_bias_qv, grad_bias_proj, gra...]
    reduce_sum x15 -> x0, other arithmetic: 37.6 us -> none  [the longest x4 18.1 us: norm_apply(): return offset * lax.rsqrt(spread + eps_norm) * norm_gain + norm_shift]
    another operation x13 -> x10, local copies, waits for them, and re-layouts: 24.4 us -> 4.87 us  [the longest x9 4.87 us: body(): jnp.stack([ln1_gain, ln1_bias, bias_proj, ln2_gain, ln2_bias, bias_fc1, b...]
  transfers between devices with their start and end apart: 8 -> 0, of which waited for: 8 -> 0; matrix products, arithmetic and copies ran while one was open for 5% -> 0% of each run, Pallas kernels for 0% -> 0%
where the time goes in v1:
time: 203 us; the launch traced here: 199 us
  Pallas kernels  175 us (86%)
  local copies, waits for them, and re-layouts  22.9 us (11%)
    pallas_call x1, Pallas kernels, body(): pl.pallas_call(functools.partial(kernel, cfg), out_shape=[sds((rows, D),...  175 us
    unnamed x16, local copies, waits for them, and re-layouts  11.9 us
    another operation x9, local copies, waits for them, and re-layouts, body(): jnp.stack([ln1_gain, ln1_bias, bias_proj, ln2_gain, ln2_bias, bias_fc1, b...  4.87 us

profile of v1, /device:TPU:0, one launch (start us, length us, event | category | flops | bytes accessed | tf_op | source)
XLA Modules:
  0.0 199.4 jit_solution(2561249485455192358)
XLA Ops:
  0.6 0.8 slice_reduce_fusion.1
  1.5 0.7 stack.30
  2.1 0.7 stack.31
  2.8 0.7 stack.32
  3.5 0.7 stack.33
  4.2 0.7 stack.34
  4.9 0.7 stack.35
  5.6 0.7 stack.36
  6.3 0.1 stack.38
  6.3 0.6 convert_element_type.3.vec_ref
  6.9 1.7 copy.35
  8.7 1.6 copy.36.wqkv_in
  10.2 174.6 %layer.1 = (bf16[960,1024]{1,0:T(8,128)(2,1)}, f32[960,1024]{1,0:T(8,128)}, f32[3]{0:T(128)}, f32[8,1024]{1,0:T(8,128)}, f32[128,1024]{1,0:T(8,128)}, /*index=5*...) custom-call(s32[24]{0:T(128)} %kept_ref.1, f32[8,1024]{1,0:T(8,128)} %convert_element_type.3.vec_ref, ...), custom_call_target="tpu_custom_call" | custom-call | tf_op jit(solution)/shard_map/layer/pallas_call | solution.py:560
  184.9 0.0 copy-start.1
  184.9 0.9 fusion.1
  185.7 1.8 fusion
  187.5 0.6 pad_maximum_fusion.1
  188.1 1.7 copy.39
  189.7 1.1 copy.37
  190.9 0.9 copy.38
  191.8 0.0 copy-start.3
  191.8 2.0 %copy.40 = f32[1024,128]{1,0:T(8,128)} copy(f32[1024,128]{0,1:T(8,128)} %bitcast.13) | data formatting | bytes 1048576
  193.9 0.0 copy-done.1
  193.9 0.0 copy-start
  193.9 1.3 copy.45
  195.1 0.0 copy-done.3
  195.1 0.5 copy.46
  195.7 1.0 copy-done
  196.7 0.0 copy-start.2
  196.7 1.9 copy.47
  198.6 0.0 copy-done.2
  198.6 0.8 copy.48
  (3 shorter events, 0.0 us)
Async XLA Ops:
  184.9 9.0 %copy-start.1 = (bf16[960,1024]{1,0:T(8,128)(2,1)S(1)}, bf16[960,1024]{1,0:T(8,128)(2,1)}, u32[]{:S(2)}) copy-start(bf16[960,1024]{1,0:T(8,128)(2,1)} %get-tuple-element.87) | copy-start | bytes 5898244
  191.8 3.3 %copy-start.3 = (f32[3]{0:T(128)S(1)}, f32[3]{0:T(128)}, u32[]{:S(2)}) copy-start(f32[3]{0:T(128)} %get-tuple-element.88) | copy-start | bytes 40
  193.9 2.8 %copy-start = (f32[960,1024]{1,0:T(8,128)S(1)}, f32[960,1024]{1,0:T(8,128)}, u32[]{:S(2)}) copy-start(f32[960,1024]{1,0:T(8,128)} %get-tuple-element.89) | copy-start | bytes 11796484
  196.7 1.9 copy-start.2

commit v2 on v1

--- a/solution.py
+++ b/solution.py
@@ -35,56 +35,57 @@
 
 def kernel(
     cfg,
-    kept_ref, vec_ref, tok_in, tea_in, og_in, wqkv_in, wproj_in, wfc1_in, wfc2_in,
-    out_hbm, tg_hbm, loss_ref, vout_ref, gfc2_ref, gfc1_ref, gproj_ref, gqkv_ref,
+    kept_ref, ln1g_in, ln1b_in, bproj_in, ln2g_in, ln2b_in, bfc1_in, bfc2_in, bqv_in,
+    tok_in, tea_in, og_in, wqkv_in, wproj_in, wfc1_in, wfc2_in,
+    out_hbm, tg_hbm, loss_ref, vout_ref, gfc2_hbm, gfc1_hbm, gproj_hbm, gqkv_hbm,
     wqkv, wproj, wfc1, wfc2, tok, tea, og,
     a_r, qkv_r, heads_r, c_r, h1_r, act_r, gp_r, seed_r, sl_r, dpre_r, dqkv_r,
-    core_s, core_r, tot, gs, yr, zr, lacc, vacc, vs, vyr, vzr,
-    in_sem, out_sem, ps_s, ps_r, y_s, y_r, z_s, z_r, v_s, v_r,
+    core_s, core_r, tot, gs, rb, gfc2_r, gfc1_r, gproj_r, gqkv_r, vec_ref, lacc, vacc, vst, vrc,
+    in_sem, out_sem, ps_s, ps_r, g_s, g_r, v_s, v_r,
 ):
-    S, NZ, CH, MB, NBLK, NZB, FW = cfg
+    S, NDP, NBITS, CH, FW = cfg
     LW = wproj.shape[0]
     R = SLOTS
     rows_all = S * R
     dp = lax.axis_index("dp")
     t = lax.axis_index("tensor")
-    y = lax.rem(dp, 2)
-    z = dp // 2
     lo = lax.rem(t, 2)
     hi = t // 2
     sib = (dp, hi * 2 + (1 - lo))
     xn = (dp, (1 - hi) * 2 + lo)
-    yn = (z * 2 + (1 - y), t)
-
-    def zn(zz):
-        return (zz * 2 + y, t)
+    bits = [lax.rem(dp // (1 << b), 2) for b in range(NBITS)]
+
+    def flip(b):
+        return (dp + (1 << b) * (1 - 2 * bits[b]), t)
+
+    bar = pltpu.get_barrier_semaphore()
+    for peer in [sib, xn] + [flip(b) for b in range(NBITS)]:
+        pl.semaphore_signal(bar, inc=1, device_id=peer, device_id_type=MESH)
 
     def in_copy(i, src, dst):
         return pltpu.make_async_copy(src, dst, in_sem.at[i])
 
+    def tok_copy(s):
+        rows = pl.ds(pl.multiple_of(s * R, 64), R)
+        return pltpu.make_async_copy(tok_in.at[rows, :], tok.at[rows, :], in_sem.at[6 + s])
+
     ins = [
-        in_copy(0, tok_in, tok),
-        in_copy(1, wqkv_in, wqkv),
-        in_copy(2, wproj_in, wproj),
-        in_copy(3, wfc1_in, wfc1),
-        in_copy(4, wfc2_in, wfc2),
-        in_copy(5, tea_in, tea),
-        in_copy(6, og_in, og),
+        in_copy(0, wqkv_in, wqkv),
+        in_copy(1, wproj_in, wproj),
+        in_copy(2, wfc1_in, wfc1),
+        in_copy(3, wfc2_in, wfc2),
+        in_copy(4, tea_in, tea),
+        in_copy(5, og_in, og),
     ]
-    for c in ins:
-        c.start()
-
-    bar = pltpu.get_barrier_semaphore()
-    for peer in (sib, xn, yn):
-        pl.semaphore_signal(bar, inc=1, device_id=peer, device_id_type=MESH)
-
-    def bar_z(k, _):
-        pl.semaphore_signal(bar, inc=1, device_id=zn(lax.rem(z + k, NZ)), device_id_type=MESH)
-        return 0
-
-    lax.fori_loop(1, NZ, bar_z, 0)
-    pl.semaphore_wait(bar, 3 + NZ - 1)
-
+    tok_copy(0).start()
+    ins[0].start()
+    ins[1].start()
+    for j, ref in enumerate([ln1g_in, ln1b_in, bproj_in, ln2g_in, ln2b_in, bfc1_in, bfc2_in]):
+        vec_ref[j:j + 1, :] = ref[...].astype(F32).reshape(1, ref.shape[0])
+    vec_ref[7:8, :] = jnp.zeros((1, D), F32)
+    bqv = bqv_in[...].astype(F32)
+    vec_ref[7:8, 0:LW] = bqv[0:1]
+    vec_ref[7:8, 2 * LW:3 * LW] = bqv[1:2]
     vacc[...] = jnp.zeros_like(vacc)
     count = lax.fori_loop(
         0, kept_ref.shape[0], lambda i, acc: acc + (kept_ref[i] + BUFFER).astype(F32), jnp.float32(0.0)
@@ -101,7 +102,7 @@
         return pl.ds(pl.multiple_of(s * R, 64), R)
 
     def chunks(fn, init=0):
-        return lax.fori_loop(0, R // RB, fn, init)
+        return lax.fori_loop(0, R // RB, fn, init, unroll=2)
 
     def blk(s, i):
         return pl.ds(pl.multiple_of(s * R + i * RB, RB), RB)
@@ -182,11 +183,120 @@
 
     npair = LW // (2 * HEAD)
 
-    ins[0].wait()
-    ins[1].wait()
-    ins[2].wait()
+    def swapped(tile):
+        return (3 - lax.rem(tile + 3, 4)) // 3 if NBITS > 1 else 0
+
+    def mix(f, p, q):
+        return p + f * (q - p)
+
+    def place(d, f):
+        db = [(d >> b) & 1 for b in range(NBITS)]
+        pos = sum(db[b] << (NBITS - 1 - b) for b in range(2, NBITS))
+        if NBITS > 1:
+            return pos + mix(f, db[0], db[1]) * (NDP // 2) + mix(f, db[1], db[0]) * (NDP // 4)
+        return db[0]
+
+    def stage_bit(f, j):
+        if NBITS > 1 and j < 2:
+            return mix(f, bits[j], bits[1 - j])
+        return bits[j]
+
+    def stage_peer(f, j):
+        if NBITS > 1 and j < 2:
+            step = [(1 << b) * (1 - 2 * bits[b]) for b in range(2)]
+            return (dp + mix(f, step[j], step[1 - j]), t)
+        return flip(j)
+
+    def base(f, j):
+        return sum((stage_bit(f, i) * (NDP >> (i + 1)) for i in range(j)), 0)
+
+    def land(j):
+        return NDP - (NDP >> j)
+
+    def cp_g(tile, j):
+        f = swapped(tile)
+        n = NDP >> (j + 1)
+        first = base(f, j) + (1 - stage_bit(f, j)) * n
+        return pltpu.make_async_remote_copy(
+            src_ref=gs.at[tile, pl.ds(first, n)], dst_ref=rb.at[tile, land(j):land(j) + n],
+            send_sem=g_s.at[tile, j], recv_sem=g_r.at[tile, j],
+            device_id=stage_peer(f, j), device_id_type=MESH,
+        )
+
+    def grad_tile(tile, lhs, rhs):
+        f = swapped(tile)
+        val = mm(lhs[...], rhs, TN).astype(BF16)
+        for d in range(NDP):
+            gs[tile, place(d, f)] = val[d * CH:(d + 1) * CH]
+        cp_g(tile, 0).start()
+
+    def grad_tiles(first, last, lhs, rhs, skip=0):
+        def one(k, _):
+            grad_tile(k, lhs, rhs[:, pl.ds(pl.multiple_of((k - skip) * 256, 256), 256)])
+            return 0
+
+        lax.fori_loop(first, last, one, 0)
+
+    def advance(tile, j):
+        f = swapped(tile)
+        cp_g(tile, j).wait_recv()
+        n = NDP >> (j + 1)
+        mine = base(f, j + 1)
+
+        if j + 1 < NBITS:
+            def add(i, _):
+                gs[tile, mine + i] = gs[tile, mine + i] + rb[tile, land(j) + i]
+                return 0
+
+            lax.fori_loop(0, n, add, 0)
+            cp_g(tile, j + 1).start()
+            return
+        val = gs[tile, mine].astype(F32) + rb[tile, land(j)].astype(F32)
+
+        def cols(k):
+            return pl.ds(pl.multiple_of(k * 256, 256), 256)
+
+        @pl.when(tile < NT1)
+        def _():
+            gfc2_r[cols(tile), :] = val.T
+
+        @pl.when(jnp.logical_and(tile >= NT1, tile < 2 * NT1))
+        def _():
+            gfc1_r[:, cols(tile - NT1)] = val
+
+        @pl.when(jnp.logical_and(tile >= 2 * NT1, tile < 2 * NT1 + NT2))
+        def _():
+            gproj_r[cols(tile - 2 * NT1), :] = val.T
+
+        @pl.when(tile >= 2 * NT1 + NT2)
+        def _():
+            k = tile - 2 * NT1 - NT2
+            gqkv_r[k // NT2, :, cols(lax.rem(k, NT2))] = val
+
+    def plain(u):
+        return u + (u + 2) // 3
+
+    def pump(u):
+        for j in range(NBITS):
+            @pl.when(jnp.logical_and(u - j >= 0, u - j < NX))
+            def _():
+                advance(plain(u - j), j)
+
+    def pumps(first, last):
+        def one(u, _):
+            pump(u)
+            return 0
+
+        lax.fori_loop(first, last, one, 0)
+
+    NT1 = FW // 256
+    NT2 = LW // 256
+    T = 2 * NT1 + 4 * NT2
+    NX = 3 * T // 4
 
     def phase_a(s, _):
+        tok_copy(s).wait()
+
         def ln(i, _):
             x = tok[blk(s, i), :].astype(F32) * mask_rows(s, i)
             hat, _r = norm_stats(x)
@@ -194,11 +304,24 @@
             return 0
 
         chunks(ln)
+
+        @pl.when(s == 0)
+        def _():
+            ins[0].wait()
+
+            def tok_start(i, _):
+                tok_copy(i).start()
+                return 0
+
+            lax.fori_loop(1, S, tok_start, 0)
+            for c in ins[2:]:
+                c.start()
+
         rs = seq_rows(s)
         av = a_r[rs, :]
         for c in range(3):
             cs = slice(c * LW, (c + 1) * LW)
-            qkv_r[rs, cs] = (mm(av, wqkv[:, cs], NN) + vec_ref[7:8, cs]).astype(BF16)
+            qkv_r[rs, cs] = (mm(av, wqkv[c], NN) + vec_ref[7:8, cs]).astype(BF16)
 
         def pair(hp, _):
             q = qkv_r[rs, pair_cols(0, hp)]
@@ -214,13 +337,19 @@
 
         lax.fori_loop(0, npair, pair, 0)
         hv = heads_r[rs, :]
+
+        @pl.when(s == 0)
+        def _():
+            ins[1].wait()
+            pl.semaphore_wait(bar, 2 + NBITS)
+
         ps_start(0, s, lambda h: mm(hv, wproj[:, half_cols(h)], NN))
         return 0
 
     lax.fori_loop(0, S, phase_a, 0)
 
+    ins[2].wait()
     ins[3].wait()
-    ins[4].wait()
 
     def phase_b(s, _):
         ps_finish(0, s)
@@ -251,8 +380,8 @@
 
     lax.fori_loop(0, S, phase_b, 0)
 
+    ins[4].wait()
     ins[5].wait()
-    ins[6].wait()
     loss_scale = kept_ref.shape[0] / (2.0 * count * D)
     seed_scale = kept_ref.shape[0] * SLOTS * 1.0 / count
 
@@ -284,6 +413,11 @@
         rs = seq_rows(s)
         sv = sl_r[rs, :]
 
+        @pl.when(s == S - 1)
+        def _():
+            grad_tiles(0, 2, sl_r, act_r)
+
+
         def dact(j, _):
             cs = pl.ds(pl.multiple_of(j * 256, 256), 256)
             d = mm(sv, wfc2[cs, :], NT) * gp_r[rs, cs]
@@ -298,86 +432,8 @@
 
     lax.fori_loop(0, S, phase_c, 0)
 
-    def block_at(k):
-        return lax.rem(z // NZB + 1 + k, NBLK)
-
-    def cp_y(tile):
-        return pltpu.make_async_remote_copy(
-            src_ref=gs.at[tile, :, 1 - y], dst_ref=yr.at[tile],
-            send_sem=y_s.at[tile], recv_sem=y_r.at[tile], device_id=yn, device_id_type=MESH,
-        )
-
-    def cp_z(g, tile, i, zz):
-        slot = lax.rem(zz - z + NZ, NZ) - 1
-        return pltpu.make_async_remote_copy(
-            src_ref=yr.at[tile, i], dst_ref=zr.at[g, slot],
-            send_sem=z_s.at[tile, i], recv_sem=z_r.at[g, slot], device_id=zn(zz), device_id_type=MESH,
-        )
-
-    def grad_tiles(g, lhs, parts):
-        def one(k, _):
-            cols = pl.ds(pl.multiple_of(block_at(k) * MB, MB), MB)
-            tile = g * NBLK + k
-            off = 0
-            for lref, rref in parts:
-                n = rref.shape[1]
-                val = mm(lref[:, cols], rref[...], TN)
-                gs[tile, :, :, :, off:off + n] = val.astype(BF16).reshape(NZB, 2, CH, n)
-                off += n
-            cp_y(tile).start()
-            return 0
-
-        lax.fori_loop(0, NBLK, one, 0)
-
-    def z_stage(g, k):
-        tile = g * NBLK + k
-        cp_y(tile).wait_recv()
-
-        def one(i, _):
-            zz = block_at(k) * NZB + i
-            yr[tile, i] = (gs[tile, i, y].astype(F32) + yr[tile, i].astype(F32)).astype(BF16)
-
-            @pl.when(zz != z)
-            def _():
-                cp_z(g, tile, i, zz).start()
-
-            return 0
-
-        lax.fori_loop(0, NZB, one, 0)
-
-    def z_stages(g):
-        def one(k, _):
-            z_stage(g, k)
-            return 0
-
-        lax.fori_loop(0, NBLK, one, 0)
-
-    def grad_final(g, outs):
-        def wait(j, _):
-            zz = lax.rem(z + 1 + j, NZ)
-            pltpu.make_async_remote_copy(
-                src_ref=yr.at[0, 0], dst_ref=zr.at[g, j], send_sem=z_s.at[0, 0],
-                recv_sem=z_r.at[g, j], device_id=zn(zz), device_id_type=MESH,
-            ).wait_recv()
-            return 0
-
-        lax.fori_loop(0, NZ - 1, wait, 0)
-        own_tile = g * NBLK + NBLK - 1
-        own_i = lax.rem(z, NZB)
-        off = 0
-        for ref in outs:
-            n = ref.shape[1]
-            ref[...] = yr[own_tile, own_i, :, off:off + n].astype(F32)
-
-            def add(j, _):
-                ref[...] += zr[g, j, :, off:off + n].astype(F32)
-                return 0
-
-            lax.fori_loop(0, NZ - 1, add, 0)
-            off += n
-
-    grad_tiles(0, sl_r, [(sl_r, act_r)])
-    grad_tiles(1, c_r, [(c_r, dpre_r)])
+    grad_tiles(2, NT1, sl_r, act_r)
+    grad_tiles(NT1, 2 * NT1, c_r, dpre_r, NT1)
 
     def phase_d(s, _):
         ps_finish(0, s)
@@ -427,12 +483,21 @@
             return 0
 
         lax.fori_loop(0, npair, pair, 0)
-        ps_start(1, s, lambda h: mm(dqkv_r[rs, :], wqkv[half_cols(h), :], NT))
+        ps_start(1, s, lambda h: sum(
+            mm(dqkv_r[rs, c * LW:(c + 1) * LW], wqkv[c, half_cols(h), :], NT) for c in range(3)
+        ))
+        @pl.when(s < 2)
+        def _():
+            advance(4 * s + 1, 0)
+
+        pump(s)
         return 0
 
     lax.fori_loop(0, S, phase_d, 0)
-    grad_tiles(2, None, [(sl_r, heads_r), (a_r, dqkv_r)])
-    z_stages(0)
+    grad_tiles(2 * NT1, 2 * NT1 + LW // 256, sl_r, heads_r, 2 * NT1)
+    grad_tiles(2 * NT1 + LW // 256, T, a_r, dqkv_r, 2 * NT1 + LW // 256)
+
+    pump(S)
 
     def phase_e(s, _):
         ps_finish(1, s)
@@ -451,77 +516,61 @@
 
         chunks(lnb)
         tg_copy(s).start()
+        pump(S + 1 + s)
         return 0
 
     lax.fori_loop(0, S, phase_e, 0)
 
     for j in range(8):
-        vs[j:j + 1, :] = jnp.sum(vacc[j], axis=0, keepdims=True)
-    vy = pltpu.make_async_remote_copy(
-        src_ref=vs, dst_ref=vyr, send_sem=v_s.at[0], recv_sem=v_r.at[0], device_id=yn, device_id_type=MESH
-    )
-    vy.start()
-
-    z_stages(1)
-    vy.wait()
-    vzr[z] = vs[...] + vyr[...]
-
-    def cp_v(k, zz):
+        vst[0, j:j + 1, :] = jnp.sum(vacc[j], axis=0, keepdims=True)
+
+    def cp_v(j):
         return pltpu.make_async_remote_copy(
-            src_ref=vzr.at[z], dst_ref=vzr.at[z], send_sem=v_s.at[k], recv_sem=v_r.at[k],
-            device_id=zn(zz), device_id_type=MESH,
+            src_ref=vst.at[j], dst_ref=vrc.at[j], send_sem=v_s.at[j], recv_sem=v_r.at[j],
+            device_id=flip(j), device_id_type=MESH,
         )
 
-    def v_go(k, _):
-        cp_v(k, lax.rem(z + k, NZ)).start()
+    def step_v(j):
+        cp_v(j).wait()
+        total = vst[j] + vrc[j]
+        if j + 1 < NBITS:
+            vst[j + 1] = total
+            cp_v(j + 1).start()
+        else:
+            vout_ref[...] = total
+
+    cp_v(0).start()
+    advance(9, 0)
+    advance(1, 1)
+    advance(5, 1)
+    step_v(0)
+    pump(2 * S + 1)
+    step_v(1)
+    for j in range(2, NBITS):
+        advance(1, j)
+        advance(5, j)
+    pump(2 * S + 2)
+    for j in range(2, NBITS):
+        step_v(j)
+    advance(9, 1)
+    pumps(2 * S + 3, NX + NBITS - 1)
+    for j in range(2, NBITS):
+        advance(9, j)
+    grad_out = [
+        pltpu.make_async_copy(src, dst, out_sem.at[2, i])
+        for i, (src, dst) in enumerate(
+            ((gfc2_r, gfc2_hbm), (gfc1_r, gfc1_hbm), (gproj_r, gproj_hbm), (gqkv_r, gqkv_hbm))
+        )
+    ]
+    for c in grad_out:
+        c.start()
+
+    def drain(tile, _):
+        for j in range(NBITS):
+            cp_g(tile, j).wait_send()
         return 0
 
-    lax.fori_loop(1, NZ, v_go, 0)
-    z_stages(2)
-
-    def v_wait(k, _):
-        src = lax.rem(z - k + NZ, NZ)
-        c = pltpu.make_async_remote_copy(
-            src_ref=vzr.at[z], dst_ref=vzr.at[src], send_sem=v_s.at[k], recv_sem=v_r.at[k],
-            device_id=zn(lax.rem(z + k, NZ)), device_id_type=MESH,
-        )
-        c.wait_recv()
-        cp_v(k, lax.rem(z + k, NZ)).wait_send()
-        return 0
-
-    lax.fori_loop(1, NZ, v_wait, 0)
-    vout_ref[...] = jnp.zeros_like(vout_ref)
-
-    def v_add(k, _):
-        vout_ref[...] += vzr[k]
-        return 0
-
-    lax.fori_loop(0, NZ, v_add, 0)
-
-    grad_final(0, [gfc2_ref])
-    grad_final(1, [gfc1_ref])
-    grad_final(2, [gproj_ref, gqkv_ref])
-
-    def drain_y(tile, _):
-        cp_y(tile).wait_send()
-        return 0
-
-    lax.fori_loop(0, 3 * NBLK, drain_y, 0)
-    for g in range(3):
-        def drain_z(k, _):
-            def one(i, _):
-                zz = block_at(k) * NZB + i
-
-                @pl.when(zz != z)
-                def _():
-                    cp_z(g, g * NBLK + k, i, zz).wait_send()
-
-                return 0
-
-            lax.fori_loop(0, NZB, one, 0)
-            return 0
-
-        lax.fori_loop(0, NBLK, drain_z, 0)
+    lax.fori_loop(0, T, drain, 0)
 
     def drain_out(s, _):
         out_copy(s).wait()
@@ -529,6 +578,39 @@
         return 0
 
     lax.fori_loop(0, S, drain_out, 0)
+    for c in grad_out:
+        c.wait()
+
+
+def finish(loss_in, v_in, *refs):
+    ins, refs = refs[:6], refs[6:]
+    loss_o, ln1g_o, ln1b_o, bqv_o, bproj_o, ln2g_o, ln2b_o, bfc1_o, bfc2_o = refs[:9]
+    outs, mids, sem = refs[9:15], refs[15:21], refs[21]
+    moves = []
+    for src, mid, dst in zip(ins, mids, outs):
+        rows = src.shape[0]
+        parts = rows // 240 if rows % 240 == 0 else 1
+        for i in range(parts):
+            rr = pl.ds(i * (rows // parts), rows // parts)
+            k = len(moves)
+            moves.append((
+                pltpu.make_async_copy(src.at[rr], mid.at[rr], sem.at[0, k]),
+                pltpu.make_async_copy(mid.at[rr], dst.at[rr], sem.at[1, k]),
+            ))
+    for c, _ in moves:
+        c.start()
+    for i in range(loss_in.shape[0]):
+        loss_o[i] = loss_in[i]
+    for j, ref in enumerate([ln1g_o, ln1b_o, bproj_o, ln2g_o, ln2b_o, bfc1_o, bfc2_o]):
+        ref[...] = v_in[j]
+    lw = bqv_o.shape[1]
+    bqv_o[0:1, :] = v_in[7:8, 0:lw]
+    bqv_o[1:2, :] = v_in[7:8, lw:2 * lw]
+    for c, d in moves:
+        c.wait()
+        d.start()
+    for _, d in moves:
+        d.wait()
 
 
 def body(
@@ -540,54 +622,61 @@
     S = rows // SLOTS
     LW = w_qkv.shape[2]
     FW = w_fc1.shape[1]
-    NZ = n_dp // 2
     CH = D // n_dp
-    MB = max(256, 2 * CH)
-    NBLK = D // MB
-    NZB = MB // (2 * CH)
-    T = 3 * NBLK
-    cfg = (S, NZ, CH, MB, NBLK, NZB, FW)
-    qb = jnp.concatenate([bias_qv[0], jnp.zeros_like(bias_qv[0]), bias_qv[1], jnp.zeros((D - 3 * LW,), BF16)])
-    vec = jnp.stack(
-        [ln1_gain, ln1_bias, bias_proj, ln2_gain, ln2_bias, bias_fc1, bias_fc2, qb]
-    ).astype(F32)
+    NBITS = n_dp.bit_length() - 1
+    T = (2 * FW + 4 * LW) // 256
+    cfg = (S, n_dp, NBITS, CH, FW)
     any_spec = pl.BlockSpec(memory_space=pl.ANY)
     vm = pl.BlockSpec(memory_space=pltpu.VMEM)
     sm = pl.BlockSpec(memory_space=pltpu.SMEM)
     sds = jax.ShapeDtypeStruct
     DMA = pltpu.SemaphoreType.DMA
     V = pltpu.VMEM
-    out, token_grad, loss, vout, gfc2, gfc1, gproj, gqkv = pl.pallas_call(
+    big = [
+        ((rows, D), BF16), ((rows, D), F32), ((FW, CH), F32), ((CH, FW), F32), ((LW, CH), F32), ((3, CH, LW), F32),
+    ]
+    out, tg, loss, vout, *grads = pl.pallas_call(
         functools.partial(kernel, cfg),
-        out_shape=[
-            sds((rows, D), BF16), sds((rows, D), F32), sds((S,), F32), sds((8, D), F32),
-            sds((CH, FW), F32), sds((CH, FW), F32), sds((CH, LW), F32), sds((CH, 3 * LW), F32),
-        ],
-        in_specs=[sm, vm] + [any_spec] * 7,
-        out_specs=[any_spec, any_spec, sm] + [vm] * 5,
+        out_shape=[sds(*big[0]), sds(*big[1]), sds((S,), F32), sds((8, D), F32)] + [sds(*b) for b in big[2:]],
+        in_specs=[sm] + [vm] * 8 + [any_spec] * 7,
+        out_specs=[any_spec, any_spec, sm, vm] + [any_spec] * 4,
         scratch_shapes=[
-            V((D, 3 * LW), BF16), V((LW, D), BF16), V((D, FW), BF16), V((FW, D), BF16),
+            V((3, D, LW), BF16), V((LW, D), BF16), V((D, FW), BF16), V((FW, D), BF16),
             V((rows, D), BF16), V((rows, D), BF16), V((rows, D), BF16),
             V((rows, D), BF16), V((rows, 3 * LW), BF16), V((rows, LW), BF16), V((rows, D), BF16),
             V((rows, D), F32), V((rows, FW), BF16), V((rows, FW), F32), V((rows, D), F32),
             V((rows, D), BF16), V((rows, FW), BF16), V((rows, 3 * LW), BF16),
             V((S, SLOTS, HALF), BF16), V((S, SLOTS, HALF), BF16), V((2, S, 2, 2, SLOTS, HALF), BF16),
-            V((T, NZB, 2, CH, 1024), BF16), V((T, NZB, CH, 1024), BF16), V((3, NZ - 1, CH, 1024), BF16),
-            V((8, D), F32), V((8, 8, D), F32), V((8, D), F32), V((8, D), F32), V((NZ, 8, D), F32),
-            DMA((7,)), DMA((2, S)), DMA((2, S, 4)), DMA((2, S, 4)), DMA((T,)), DMA((T,)),
-            DMA((T, NZB)), DMA((3, NZ - 1)), DMA((NZ,)), DMA((NZ,)),
+            V((T, n_dp, CH, 256), BF16), V((T, n_dp - 1, CH, 256), BF16),
+            V((FW, CH), F32), V((CH, FW), F32), V((LW, CH), F32), V((3, CH, LW), F32),
+            V((8, D), F32), V((8, D), F32), V((8, 8, D), F32), V((NBITS, 8, D), F32), V((NBITS, 8, D), F32),
+            DMA((6 + S,)), DMA((3, max(S, 4))), DMA((2, S, 4)), DMA((2, S, 4)), DMA((T, NBITS)), DMA((T, NBITS)),
+            DMA((NBITS,)), DMA((NBITS,)),
         ],
         compiler_params=pltpu.CompilerParams(
             collective_id=0, has_side_effects=True, vmem_limit_bytes=64 * 2**20 - 2**18
         ),
         name="layer",
     )(
-        kept, vec, tokens, teacher, out_grad, w_qkv.reshape(D, 3 * LW), w_proj, w_fc1, w_fc2,
+        kept, ln1_gain, ln1_bias, bias_proj, ln2_gain, ln2_bias, bias_fc1, bias_fc2, bias_qv,
+        tokens, teacher, out_grad, w_qkv.transpose(1, 0, 2), w_proj, w_fc1, w_fc2,
+    )
+    vd = sds((D,), F32)
+    loss, g_ln1g, g_ln1b, g_bqv, g_bproj, g_ln2g, g_ln2b, g_bfc1, g_bfc2, out, token_grad, g_wfc2, g_wfc1, g_wproj, g_wqkv = (
+        pl.pallas_call(
+            finish,
+            out_shape=[sds((S,), F32), vd, vd, sds((2, LW), F32), vd, vd, vd, sds((FW,), F32), vd]
+            + [sds(*b) for b in big],
+            in_specs=[sm, vm] + [any_spec] * 6,
+            out_specs=[sm] + [vm] * 8 + [any_spec] * 6,
+            scratch_shapes=[V(*b) for b in big] + [DMA((2, 16))],
+            compiler_params=pltpu.CompilerParams(vmem_limit_bytes=60 * 2**20),
+            name="finish",
+        )(loss, vout, out, tg, *grads)
     )
     return (
-        out, loss, token_grad, vout[0], vout[1], gqkv.reshape(CH, 3, LW),
-        jnp.stack([vout[7, :LW], vout[7, LW:2 * LW]]), gproj.T, vout[2], vout[3], vout[4],
-        gfc1, vout[5], gfc2.T, vout[6],
+        out, loss, token_grad, g_ln1g, g_ln1b, g_wqkv.transpose(1, 0, 2), g_bqv, g_wproj, g_bproj, g_ln2g, g_ln2b,
+        g_wfc1, g_bfc1, g_wfc2, g_bfc2,
     )
 
 

time: 203 us -> 153 us (0.75); the launches traced: 199 us -> 152 us
  Pallas kernels: 175 us -> 152 us
  local copies, waits for them, and re-layouts: 22.9 us -> 0 us
    pallas_call x1 -> x2, Pallas kernels: 175 us -> 152 us  [the longest x1 144 us: body(): pl.pallas_call(functools.partial(kernel, cfg), out_shape=[sds(*big[0]), s...]
    unnamed x16 -> x0, local copies, waits for them, and re-layouts: 11.9 us -> none
    another operation x10 -> x0, local copies, waits for them, and re-layouts: 4.87 us -> none  [the longest x9 4.87 us: body(): jnp.stack([ln1_gain, ln1_bias, bias_proj, ln2_gain, ln2_bias, bias_fc1, b...]
    slice x3 -> x0, local copies, waits for them, and re-layouts: 3.41 us -> none  [the longest x1 1.78 us: body(): vout[6]]
where the time goes in v2:
time: 153 us; the launch traced here: 152 us
  Pallas kernels  152 us (99%)
    pallas_call x1, Pallas kernels, body(): pl.pallas_call(functools.partial(kernel, cfg), out_shape=[sds(*big[0]), s...  144 us
    pallas_call x1, Pallas kernels, body(): pl.pallas_call(finish, out_shape=[sds((S,), F32), vd, vd, sds((2, LW), F3...  7.31 us

profile of v2, /device:TPU:0, one launch (start us, length us, event | category | flops | bytes accessed | tf_op | source)
XLA Modules:
  0.0 152.4 jit_solution(497262229066434654)
XLA Ops:
  0.7 144.4 %layer.1 = (bf16[960,1024]{1,0:T(8,128)(2,1)}, f32[960,1024]{1,0:T(8,128)}, f32[3]{0:T(128)}, f32[8,1024]{1,0:T(8,128)}, f32[1024,128]{1,0:T(8,128)}, /*index=5*...) custom-call(s32[24]{0:T(128)} %kept_ref.1, bf16[1024]{0:T(1024)(128)(2,1)} %ln1g_in.1, ...), custom_call_target="tpu_custom_call" | custom-call | tf_op jit(solution)/shard_map/layer/pallas_call | solution.py:638
  145.1 7.3 %finish.1 = (f32[3]{0:T(128)}, f32[1024]{0:T(1024)}, f32[1024]{0:T(1024)}, f32[2,256]{1,0:T(2,128)}, f32[1024]{0:T(1024)}, /*index=5*/f32[1024]{0:T(1024)}, f32[...) custom-call(f32[3]{0:T(128)} %get-tuple-element.38.loss_in, ...), custom_call_target="tpu_custom_call" | custom-call | tf_op jit(solution)/shard_map/finish/pallas_call | solution.py:666

commit v3 on v2

--- a/solution.py
+++ b/solution.py
@@ -37,11 +37,11 @@
     cfg,
     kept_ref, ln1g_in, ln1b_in, bproj_in, ln2g_in, ln2b_in, bfc1_in, bfc2_in, bqv_in,
     tok_in, tea_in, og_in, wqkv_in, wproj_in, wfc1_in, wfc2_in,
-    out_hbm, tg_hbm, loss_ref, vout_ref, gfc2_hbm, gfc1_hbm, gproj_hbm, gqkv_hbm,
-    wqkv, wproj, wfc1, wfc2, tok, tea, og,
-    a_r, qkv_r, heads_r, c_r, h1_r, act_r, gp_r, seed_r, sl_r, dpre_r, dqkv_r,
-    core_s, core_r, tot, gs, rb, gfc2_r, gfc1_r, gproj_r, gqkv_r, vec_ref, lacc, vacc, vst, vrc,
-    in_sem, out_sem, ps_s, ps_r, g_s, g_r, v_s, v_r,
+    tea, seed_r, loss_ref, vout_ref, gfc2_r, gfc1_r, gproj_r, gqkv_r,
+    wqkv, wproj, wfc1, wfc2, tok, og,
+    a_r, qkv_r, heads_r, c_r, h1_r, act_r, gp_r, sl_r, dpre_r, dqkv_r,
+    core_s, core_r, tot, gs, rb, vec_ref, lacc, vacc, vst, vrc,
+    in_sem, ps_s, ps_r, g_s, g_r, v_s, v_r,
 ):
     S, NDP, NBITS, CH, FW = cfg
     LW = wproj.shape[0]
@@ -148,10 +148,12 @@
         cp_x(p, s).start()
         cp_f1(p, s).start()
 
-    def ps_finish(p, s):
+    def ps_forward(p, s):
         cp_core(p, s).wait_send()
         cp_x(p, s).wait()
         cp_f2(p, s).start()
+
+    def ps_finish(p, s):
         cp_f1(p, s).wait()
         cp_f2(p, s).wait()
 
@@ -184,7 +186,7 @@
     npair = LW // (2 * HEAD)
 
     def swapped(tile):
-        return (3 - lax.rem(tile + 3, 4)) // 3 if NBITS > 1 else 0
+        return lax.rem(tile, 2) * ((T - tile) // (T - 3)) if NBITS > 1 else 0
 
     def mix(f, p, q):
         return p + f * (q - p)
@@ -273,26 +275,21 @@
             k = tile - 2 * NT1 - NT2
             gqkv_r[k // NT2, :, cols(lax.rem(k, NT2))] = val
 
-    def plain(u):
-        return u + (u + 2) // 3
-
-    def pump(u):
-        for j in range(NBITS):
-            @pl.when(jnp.logical_and(u - j >= 0, u - j < NX))
-            def _():
-                advance(plain(u - j), j)
-
-    def pumps(first, last):
-        def one(u, _):
-            pump(u)
-            return 0
-
-        lax.fori_loop(first, last, one, 0)
+    def steps(*pairs):
+        for tile, j in pairs:
+            for i in range(j, NBITS if j == 2 else j + 1):
+                advance(tile, i)
+
+    def steps_at(s, *lists):
+        for at, pairs in enumerate(lists):
+            if pairs:
+                @pl.when(s == at)
+                def _():
+                    steps(*pairs)
 
     NT1 = FW // 256
     NT2 = LW // 256
     T = 2 * NT1 + 4 * NT2
-    NX = 3 * T // 4
 
     def phase_a(s, _):
         tok_copy(s).wait()
@@ -352,6 +349,7 @@
     ins[3].wait()
 
     def phase_b(s, _):
+        ps_forward(0, s)
         ps_finish(0, s)
 
         def ln(i, _):
@@ -385,13 +383,8 @@
     loss_scale = kept_ref.shape[0] / (2.0 * count * D)
     seed_scale = kept_ref.shape[0] * SLOTS * 1.0 / count
 
-    def out_copy(s):
-        return pltpu.make_async_copy(tea.at[seq_rows(s), :], out_hbm.at[seq_rows(s), :], out_sem.at[0, s])
-
-    def tg_copy(s):
-        return pltpu.make_async_copy(seed_r.at[seq_rows(s), :], tg_hbm.at[seq_rows(s), :], out_sem.at[1, s])
-
     def phase_c(s, _):
+        ps_forward(1, s)
         ps_finish(1, s)
         lacc[...] = jnp.zeros_like(lacc)
 
@@ -408,7 +401,6 @@
             return 0
 
         chunks(fin)
-        out_copy(s).start()
         loss_ref[s] = jnp.sum(lacc[...]) * loss_scale
         rs = seq_rows(s)
         sv = sl_r[rs, :]
@@ -432,10 +424,18 @@
 
     lax.fori_loop(0, S, phase_c, 0)
 
-    grad_tiles(2, NT1, sl_r, act_r)
-    grad_tiles(NT1, 2 * NT1, c_r, dpre_r, NT1)
+    grad_tiles(2, 4, sl_r, act_r)
+    grad_tiles(4, 5, c_r, dpre_r, 4)
 
     def phase_d(s, _):
+        ps_forward(0, s)
+
+        steps_at(
+            s,
+            [(0, 0)],
+            [(4, 0), (3, 0), (0, 1)],
+            [(4, 1), (1, 1), (0, 2)],
+        )
         ps_finish(0, s)
 
         def lnb(i, _):
@@ -482,24 +482,34 @@
             vacc[7, :, pair_cols(1, hp)] += fold8(dvl.astype(F32))
             return 0
 
+        steps_at(s, [], [], [(6, 0)])
         lax.fori_loop(0, npair, pair, 0)
+        steps_at(
+            s,
+            [(1, 0), (2, 0)],
+            [(5, 0), (2, 1)],
+            [(5, 1), (2, 2)],
+        )
         ps_start(1, s, lambda h: sum(
             mm(dqkv_r[rs, c * LW:(c + 1) * LW], wqkv[c, half_cols(h), :], NT) for c in range(3)
         ))
-        @pl.when(s < 2)
-        def _():
-            advance(4 * s + 1, 0)
-
-        pump(s)
+
+        @pl.when(s == 0)
+        def _():
+            grad_tiles(5, 8, c_r, dpre_r, 4)
+
         return 0
 
     lax.fori_loop(0, S, phase_d, 0)
-    grad_tiles(2 * NT1, 2 * NT1 + LW // 256, sl_r, heads_r, 2 * NT1)
-    grad_tiles(2 * NT1 + LW // 256, T, a_r, dqkv_r, 2 * NT1 + LW // 256)
-
-    pump(S)
+    grad_tiles(8, 9, sl_r, heads_r, 8)
+    grad_tiles(9, 10, a_r, dqkv_r, 9)
+    steps((7, 0))
+    grad_tiles(10, 12, a_r, dqkv_r, 9)
+    steps((6, 1), (4, 2))
 
     def phase_e(s, _):
+        ps_forward(1, s)
+        steps_at(s, [], [(8, 0), (7, 1), (3, 1)], [])
         ps_finish(1, s)
 
         def lnb(i, _):
@@ -515,8 +525,13 @@
             return 0
 
         chunks(lnb)
-        tg_copy(s).start()
-        pump(S + 1 + s)
+
+        steps_at(
+            s,
+            [(5, 2), (1, 2)],
+            [(6, 2)],
+            [(9, 0), (3, 2)],
+        )
         return 0
 
     lax.fori_loop(0, S, phase_e, 0)
@@ -527,7 +542,7 @@
     def cp_v(j):
         return pltpu.make_async_remote_copy(
             src_ref=vst.at[j], dst_ref=vrc.at[j], send_sem=v_s.at[j], recv_sem=v_r.at[j],
-            device_id=flip(j), device_id_type=MESH,
+            device_id=flip((j + 1) % NBITS), device_id_type=MESH,
         )
 
     def step_v(j):
@@ -540,31 +555,14 @@
             vout_ref[...] = total
 
     cp_v(0).start()
-    advance(9, 0)
-    advance(1, 1)
-    advance(5, 1)
+    steps((8, 1), (7, 2))
     step_v(0)
-    pump(2 * S + 1)
-    step_v(1)
-    for j in range(2, NBITS):
-        advance(1, j)
-        advance(5, j)
-    pump(2 * S + 2)
-    for j in range(2, NBITS):
+    steps((10, 0), (9, 1), (8, 2))
+    for j in range(1, NBITS - 1):
         step_v(j)
-    advance(9, 1)
-    pumps(2 * S + 3, NX + NBITS - 1)
-    for j in range(2, NBITS):
-        advance(9, j)
-    grad_out = [
-        pltpu.make_async_copy(src, dst, out_sem.at[2, i])
-        for i, (src, dst) in enumerate(
-            ((gfc2_r, gfc2_hbm), (gfc1_r, gfc1_hbm), (gproj_r, gproj_hbm), (gqkv_r, gqkv_hbm))
-        )
-    ]
-    for c in grad_out:
-        c.start()
-
+    steps((11, 0), (10, 1), (9, 2), (11, 1))
+    step_v(NBITS - 1)
+    steps((10, 2), (11, 2))
     def drain(tile, _):
         for j in range(NBITS):
             cp_g(tile, j).wait_send()
@@ -572,32 +570,13 @@
 
     lax.fori_loop(0, T, drain, 0)
 
-    def drain_out(s, _):
-        out_copy(s).wait()
-        tg_copy(s).wait()
-        return 0
-
-    lax.fori_loop(0, S, drain_out, 0)
-    for c in grad_out:
-        c.wait()
-
 
 def finish(loss_in, v_in, *refs):
     ins, refs = refs[:6], refs[6:]
     loss_o, ln1g_o, ln1b_o, bqv_o, bproj_o, ln2g_o, ln2b_o, bfc1_o, bfc2_o = refs[:9]
-    outs, mids, sem = refs[9:15], refs[15:21], refs[21]
-    moves = []
-    for src, mid, dst in zip(ins, mids, outs):
-        rows = src.shape[0]
-        parts = rows // 240 if rows % 240 == 0 else 1
-        for i in range(parts):
-            rr = pl.ds(i * (rows // parts), rows // parts)
-            k = len(moves)
-            moves.append((
-                pltpu.make_async_copy(src.at[rr], mid.at[rr], sem.at[0, k]),
-                pltpu.make_async_copy(mid.at[rr], dst.at[rr], sem.at[1, k]),
-            ))
-    for c, _ in moves:
+    outs, sem = refs[9:15], refs[15]
+    moves = [pltpu.make_async_copy(src, dst, sem.at[i]) for i, (src, dst) in enumerate(zip(ins, outs))]
+    for c in moves:
         c.start()
     for i in range(loss_in.shape[0]):
         loss_o[i] = loss_in[i]
@@ -606,11 +585,8 @@
     lw = bqv_o.shape[1]
     bqv_o[0:1, :] = v_in[7:8, 0:lw]
     bqv_o[1:2, :] = v_in[7:8, lw:2 * lw]
-    for c, d in moves:
+    for c in moves:
         c.wait()
-        d.start()
-    for _, d in moves:
-        d.wait()
 
 
 def body(
@@ -637,24 +613,23 @@
     ]
     out, tg, loss, vout, *grads = pl.pallas_call(
         functools.partial(kernel, cfg),
-        out_shape=[sds(*big[0]), sds(*big[1]), sds((S,), F32), sds((8, D), F32)] + [sds(*b) for b in big[2:]],
+        out_shape=[V(*big[0]), V(*big[1]), sds((S,), F32), V((8, D), F32)] + [V(*b) for b in big[2:]],
         in_specs=[sm] + [vm] * 8 + [any_spec] * 7,
-        out_specs=[any_spec, any_spec, sm, vm] + [any_spec] * 4,
+        out_specs=[vm, vm, sm, vm] + [vm] * 4,
         scratch_shapes=[
             V((3, D, LW), BF16), V((LW, D), BF16), V((D, FW), BF16), V((FW, D), BF16),
-            V((rows, D), BF16), V((rows, D), BF16), V((rows, D), BF16),
+            V((rows, D), BF16), V((rows, D), BF16),
             V((rows, D), BF16), V((rows, 3 * LW), BF16), V((rows, LW), BF16), V((rows, D), BF16),
-            V((rows, D), F32), V((rows, FW), BF16), V((rows, FW), F32), V((rows, D), F32),
+            V((rows, D), F32), V((rows, FW), BF16), V((rows, FW), F32),
             V((rows, D), BF16), V((rows, FW), BF16), V((rows, 3 * LW), BF16),
             V((S, SLOTS, HALF), BF16), V((S, SLOTS, HALF), BF16), V((2, S, 2, 2, SLOTS, HALF), BF16),
             V((T, n_dp, CH, 256), BF16), V((T, n_dp - 1, CH, 256), BF16),
-            V((FW, CH), F32), V((CH, FW), F32), V((LW, CH), F32), V((3, CH, LW), F32),
             V((8, D), F32), V((8, D), F32), V((8, 8, D), F32), V((NBITS, 8, D), F32), V((NBITS, 8, D), F32),
-            DMA((6 + S,)), DMA((3, max(S, 4))), DMA((2, S, 4)), DMA((2, S, 4)), DMA((T, NBITS)), DMA((T, NBITS)),
+            DMA((6 + S,)), DMA((2, S, 4)), DMA((2, S, 4)), DMA((T, NBITS)), DMA((T, NBITS)),
             DMA((NBITS,)), DMA((NBITS,)),
         ],
         compiler_params=pltpu.CompilerParams(
-            collective_id=0, has_side_effects=True, vmem_limit_bytes=64 * 2**20 - 2**18
+            collective_id=0, has_side_effects=True, vmem_limit_bytes=56 * 2**20
         ),
         name="layer",
     )(
@@ -667,10 +642,10 @@
             finish,
             out_shape=[sds((S,), F32), vd, vd, sds((2, LW), F32), vd, vd, vd, sds((FW,), F32), vd]
             + [sds(*b) for b in big],
-            in_specs=[sm, vm] + [any_spec] * 6,
+            in_specs=[sm, vm] + [vm] * 6,
             out_specs=[sm] + [vm] * 8 + [any_spec] * 6,
-            scratch_shapes=[V(*b) for b in big] + [DMA((2, 16))],
-            compiler_params=pltpu.CompilerParams(vmem_limit_bytes=60 * 2**20),
+            scratch_shapes=[DMA((6,))],
+            compiler_params=pltpu.CompilerParams(vmem_limit_bytes=16 * 2**20),
             name="finish",
         )(loss, vout, out, tg, *grads)
     )

time: 153 us -> 140 us (0.915)
  Pallas kernels: 152 us -> 139 us
    pallas_call x1, Pallas kernels: 144 us -> 135 us  [body(): pl.pallas_call(functools.partial(kernel, cfg), out_shape=[V(*big[0]), V(*...]
    pallas_call x1, Pallas kernels: 7.31 us -> 4.26 us  [body(): pl.pallas_call(finish, out_shape=[sds((S,), F32), vd, vd, sds((2, LW), F3...]
where the time goes in v3:
time: 140 us
  Pallas kernels  139 us (99%)
    pallas_call x1, Pallas kernels, body(): pl.pallas_call(functools.partial(kernel, cfg), out_shape=[V(*big[0]), V(*...  135 us
    pallas_call x1, Pallas kernels, body(): pl.pallas_call(finish, out_shape=[sds((S,), F32), vd, vd, sds((2, LW), F3...  4.26 us

profile of v3, /device:TPU:0, one launch (start us, length us, event | category | flops | bytes accessed | tf_op | source)
XLA Modules:
  0.0 140.2 jit_solution(12953465353455461797)
XLA Ops:
  0.7 134.6 %layer.1 = (bf16[960,1024]{1,0:T(8,128)(2,1)S(1)}, f32[960,1024]{1,0:T(8,128)S(1)}, f32[3]{0:T(128)}, f32[8,1024]{1,0:T(8,128)S(1)}, f32[1024,128]{1,0:T(8,128)S...) custom-call(s32[24]{0:T(128)} %kept_ref.1, bf16[1024]{0:T(1024)(128)(2,1)} %ln1g_in.1, ...), custom_call_target="tpu_custom_call" | custom-call | tf_op jit(solution)/shard_map/layer/pallas_call | solution.py:614
  135.2 0.0 copy-start
  135.2 0.7 copy-done
  135.9 4.3 %finish.1 = (f32[3]{0:T(128)}, f32[1024]{0:T(1024)}, f32[1024]{0:T(1024)}, f32[2,256]{1,0:T(2,128)}, f32[1024]{0:T(1024)}, /*index=5*/f32[1024]{0:T(1024)}, f32[...) custom-call(f32[3]{0:T(128)S(1)} %copy-done, ...), custom_call_target="tpu_custom_call" | custom-call | tf_op jit(solution)/shard_map/finish/pallas_call | solution.py:641
Async XLA Ops:
  135.2 0.7 copy-start

commit v4 on v3

--- a/solution.py
+++ b/solution.py
@@ -37,10 +37,10 @@
     cfg,
     kept_ref, ln1g_in, ln1b_in, bproj_in, ln2g_in, ln2b_in, bfc1_in, bfc2_in, bqv_in,
     tok_in, tea_in, og_in, wqkv_in, wproj_in, wfc1_in, wfc2_in,
-    tea, seed_r, loss_ref, vout_ref, gfc2_r, gfc1_r, gproj_r, gqkv_r,
+    tea, seed_r, vout_ref, gfc2_r, gfc1_r, gproj_r, gqkv_r,
     wqkv, wproj, wfc1, wfc2, tok, og,
     a_r, qkv_r, heads_r, c_r, h1_r, act_r, gp_r, sl_r, dpre_r, dqkv_r,
-    core_s, core_r, tot, gs, rb, vec_ref, lacc, vacc, vst, vrc,
+    core_s, core_r, tot, gs, rb, vec_ref, lacc, loss_r, vacc, vst, vrc,
     in_sem, ps_s, ps_r, g_s, g_r, v_s, v_r,
 ):
     S, NDP, NBITS, CH, FW = cfg
@@ -102,7 +102,7 @@
         return pl.ds(pl.multiple_of(s * R, 64), R)
 
     def chunks(fn, init=0):
-        return lax.fori_loop(0, R // RB, fn, init, unroll=2)
+        return lax.fori_loop(0, R // RB, fn, init, unroll=5)
 
     def blk(s, i):
         return pl.ds(pl.multiple_of(s * R + i * RB, RB), RB)
@@ -169,24 +169,28 @@
 
     lane_half = lax.broadcasted_iota(jnp.int32, (1, 2 * HEAD), 1) // HEAD
 
-    def head_mask(hh):
-        return (lane_half == hh).astype(F32).astype(BF16)
+    def head_mask(hh, scale=1.0):
+        return ((lane_half == hh).astype(F32) * scale).astype(BF16)
+
+    SCALE = HEAD ** -0.5
 
     def pair_cols(c, hp):
         return pl.ds(pl.multiple_of(c * LW + hp * 2 * HEAD, 2 * HEAD), 2 * HEAD)
 
     def probs_of(qm, k, s):
-        sc = mm(qm, k, NT) * (HEAD ** -0.5)
+        sc = mm(qm, k, NT)
         col = lax.broadcasted_iota(jnp.int32, (1, R), 1)
         sc = jnp.where(col < length(s), sc, -1e30)
         top = jnp.max(sc, axis=-1, keepdims=True)
         e = jnp.exp(sc - top)
-        return e / jnp.sum(e, axis=-1, keepdims=True)
+        return e * (1.0 / jnp.sum(e, axis=-1, keepdims=True))
 
     npair = LW // (2 * HEAD)
 
     def swapped(tile):
-        return lax.rem(tile, 2) * ((T - tile) // (T - 3)) if NBITS > 1 else 0
+        if isinstance(tile, int):
+            return int(tile in (1, 3))
+        return lax.rem(tile, 2) * ((T - tile) // (T - 3))
 
     def mix(f, p, q):
         return p + f * (q - p)
@@ -215,12 +219,18 @@
     def land(j):
         return NDP - (NDP >> j)
 
+    def room(tile):
+        if isinstance(tile, int) and tile >= T - 1:
+            return T - 1, slice((tile - T + 1) * 128, (tile - T + 2) * 128)
+        return tile, slice(0, 256)
+
     def cp_g(tile, j):
         f = swapped(tile)
+        at, cols = room(tile)
         n = NDP >> (j + 1)
         first = base(f, j) + (1 - stage_bit(f, j)) * n
         return pltpu.make_async_remote_copy(
-            src_ref=gs.at[tile, pl.ds(first, n)], dst_ref=rb.at[tile, land(j):land(j) + n],
+            src_ref=gs.at[at, pl.ds(first, n), :, cols], dst_ref=rb.at[at, land(j):land(j) + n, :, cols],
             send_sem=g_s.at[tile, j], recv_sem=g_r.at[tile, j],
             device_id=stage_peer(f, j), device_id_type=MESH,
         )
@@ -231,6 +241,8 @@
         for d in range(NDP):
             gs[tile, place(d, f)] = val[d * CH:(d + 1) * CH]
         cp_g(tile, 0).start()
+        if isinstance(tile, int) and tile == T - 1:
+            cp_g(T, 0).start()
 
     def grad_tiles(first, last, lhs, rhs, skip=0):
         def one(k, _):
@@ -245,35 +257,26 @@
         n = NDP >> (j + 1)
         mine = base(f, j + 1)
 
+        at, cols = room(tile)
         if j + 1 < NBITS:
             def add(i, _):
-                gs[tile, mine + i] = gs[tile, mine + i] + rb[tile, land(j) + i]
+                gs[at, mine + i, :, cols] = gs[at, mine + i, :, cols] + rb[at, land(j) + i, :, cols]
                 return 0
 
             lax.fori_loop(0, n, add, 0)
             cp_g(tile, j + 1).start()
             return
-        val = gs[tile, mine].astype(F32) + rb[tile, land(j)].astype(F32)
-
-        def cols(k):
-            return pl.ds(pl.multiple_of(k * 256, 256), 256)
-
-        @pl.when(tile < NT1)
-        def _():
-            gfc2_r[cols(tile), :] = val.T
-
-        @pl.when(jnp.logical_and(tile >= NT1, tile < 2 * NT1))
-        def _():
-            gfc1_r[:, cols(tile - NT1)] = val
-
-        @pl.when(jnp.logical_and(tile >= 2 * NT1, tile < 2 * NT1 + NT2))
-        def _():
-            gproj_r[cols(tile - 2 * NT1), :] = val.T
-
-        @pl.when(tile >= 2 * NT1 + NT2)
-        def _():
-            k = tile - 2 * NT1 - NT2
-            gqkv_r[k // NT2, :, cols(lax.rem(k, NT2))] = val
+        val = gs[at, mine, :, cols].astype(F32) + rb[at, land(j), :, cols].astype(F32)
+        if at < NT1:
+            gfc2_r[at * 256:(at + 1) * 256, :] = val.T
+        elif at < 2 * NT1:
+            gfc1_r[:, (at - NT1) * 256:(at - NT1 + 1) * 256] = val
+        elif at < 2 * NT1 + NT2:
+            gproj_r[(at - 2 * NT1) * 256:(at - 2 * NT1 + 1) * 256, :] = val.T
+        else:
+            k = at - 2 * NT1 - NT2
+            first = (k % NT2) * 256 + cols.start
+            gqkv_r[k // NT2, :, first:first + cols.stop - cols.start] = val
 
     def steps(*pairs):
         for tile, j in pairs:
@@ -326,7 +329,7 @@
             v = qkv_r[rs, pair_cols(2, hp)]
             o = None
             for hh in range(2):
-                pr = probs_of(q * head_mask(hh), k, s).astype(BF16)
+                pr = probs_of(q * head_mask(hh, SCALE), k, s).astype(BF16)
                 oh = mm(pr, v * head_mask(hh), NN)
                 o = oh if o is None else o + oh
             heads_r[rs, pair_cols(0, hp)] = o.astype(BF16)
@@ -345,11 +348,12 @@
 
     lax.fori_loop(0, S, phase_a, 0)
 
+    ps_forward(0, 0)
+
     ins[2].wait()
     ins[3].wait()
 
     def phase_b(s, _):
-        ps_forward(0, s)
         ps_finish(0, s)
 
         def ln(i, _):
@@ -373,6 +377,14 @@
             return 0
 
         lax.fori_loop(0, FW // 256, fc1, 0)
+        @pl.when(s + 1 < S)
+        def _():
+            ps_forward(0, s + 1)
+
+        @pl.when(s + 1 == S)
+        def _():
+            ps_forward(1, 0)
+
         ps_start(1, s, lambda h: mm(act_r[rs, :], wfc2[:, half_cols(h)], NN))
         return 0
 
@@ -383,25 +395,34 @@
     loss_scale = kept_ref.shape[0] / (2.0 * count * D)
     seed_scale = kept_ref.shape[0] * SLOTS * 1.0 / count
 
+    loss_r[...] = jnp.zeros_like(loss_r)
+
     def phase_c(s, _):
-        ps_forward(1, s)
+        lacc[...] = jnp.zeros_like(lacc)
+
+        def fin(h):
+            hc = half_cols(h)
+
+            def one(i, _):
+                m = mask_rows(s, i)
+                mlp = tot[1, s, h, 0, loc(i), :].astype(F32) + tot[1, s, h, 1, loc(i), :].astype(F32)
+                final = (h1_r[blk(s, i), hc] + mlp + vec_ref[6:7, hc]) * m
+                diff = (final - tea[blk(s, i), hc].astype(F32)) * m
+                seed = (og[blk(s, i), hc].astype(F32) + diff * seed_scale) * m
+                tea[blk(s, i), hc] = final.astype(BF16)
+                seed_r[blk(s, i), hc] = seed
+                sl_r[blk(s, i), hc] = seed.astype(BF16)
+                lacc[...] += fold8(diff * diff)
+                vacc[6, :, hc] += fold8(seed)
+                return 0
+
+            chunks(one)
+
+        fin(lo)
         ps_finish(1, s)
-        lacc[...] = jnp.zeros_like(lacc)
-
-        def fin(i, _):
-            m = mask_rows(s, i)
-            final = (h1_r[blk(s, i), :] + ps_total(1, s, i) + vec_ref[6:7, :]) * m
-            diff = (final - tea[blk(s, i), :].astype(F32)) * m
-            seed = (og[blk(s, i), :].astype(F32) + diff * seed_scale) * m
-            tea[blk(s, i), :] = final.astype(BF16)
-            seed_r[blk(s, i), :] = seed
-            sl_r[blk(s, i), :] = seed.astype(BF16)
-            lacc[...] += fold8(diff * diff)
-            vacc[6] += fold8(seed)
-            return 0
-
-        chunks(fin)
-        loss_ref[s] = jnp.sum(lacc[...]) * loss_scale
+        fin(1 - lo)
+        here = (lax.broadcasted_iota(jnp.int32, (1, D), 1) == s).astype(F32)
+        loss_r[...] += here * (jnp.sum(lacc[...]) * loss_scale)
         rs = seq_rows(s)
         sv = sl_r[rs, :]
 
@@ -420,22 +441,20 @@
 
         lax.fori_loop(0, FW // 256, dact, 0)
         ps_start(0, s, lambda h: mm(dpre_r[rs, :], wfc1[half_cols(h), :], NT))
+
+        @pl.when(s + 1 < S)
+        def _():
+            ps_forward(1, s + 1)
+
         return 0
 
     lax.fori_loop(0, S, phase_c, 0)
 
     grad_tiles(2, 4, sl_r, act_r)
     grad_tiles(4, 5, c_r, dpre_r, 4)
+    ps_forward(0, 0)
 
     def phase_d(s, _):
-        ps_forward(0, s)
-
-        steps_at(
-            s,
-            [(0, 0)],
-            [(4, 0), (3, 0), (0, 1)],
-            [(4, 1), (1, 1), (0, 2)],
-        )
         ps_finish(0, s)
 
         def lnb(i, _):
@@ -464,7 +483,7 @@
             dq = dk = dv = None
             for hh in range(2):
                 hm = head_mask(hh)
-                qm, km, dm = q * hm, k * hm, dh * hm
+                qm, km, dm = q * head_mask(hh, SCALE), k * hm, dh * hm
                 pr = probs_of(qm, k, s)
                 dpr = mm(dm, v, NT)
                 ds = (pr * (dpr - jnp.sum(pr * dpr, axis=-1, keepdims=True))).astype(BF16)
@@ -473,23 +492,36 @@
                     dq, dk, dv = q1, k1, v1
                 else:
                     dq, dk, dv = dq + q1, dk + k1, dv + v1
-            dql = (dq * (HEAD ** -0.5)).astype(BF16)
+            dql = (dq * SCALE).astype(BF16)
             dvl = dv.astype(BF16)
             dqkv_r[rs, pair_cols(0, hp)] = dql
-            dqkv_r[rs, pair_cols(1, hp)] = (dk * (HEAD ** -0.5)).astype(BF16)
+            dqkv_r[rs, pair_cols(1, hp)] = dk.astype(BF16)
             dqkv_r[rs, pair_cols(2, hp)] = dvl
             vacc[7, :, pair_cols(0, hp)] += fold8(dql.astype(F32))
             vacc[7, :, pair_cols(1, hp)] += fold8(dvl.astype(F32))
             return 0
 
-        steps_at(s, [], [], [(6, 0)])
-        lax.fori_loop(0, npair, pair, 0)
+        steps_at(
+            s,
+            [(0, 0)],
+            [(4, 0), (3, 0), (0, 1)],
+            [(5, 0), (4, 1), (1, 1), (0, 2)],
+        )
+        lax.fori_loop(0, npair, pair, 0, unroll=True)
         steps_at(
             s,
             [(1, 0), (2, 0)],
-            [(5, 0), (2, 1)],
-            [(5, 1), (2, 2)],
+            [(2, 1)],
+            [(6, 0), (5, 1), (2, 2)],
         )
+        @pl.when(s + 1 < S)
+        def _():
+            ps_forward(0, s + 1)
+
+        @pl.when(s + 1 == S)
+        def _():
+            ps_forward(1, 0)
+
         ps_start(1, s, lambda h: sum(
             mm(dqkv_r[rs, c * LW:(c + 1) * LW], wqkv[c, half_cols(h), :], NT) for c in range(3)
         ))
@@ -504,11 +536,11 @@
     grad_tiles(8, 9, sl_r, heads_r, 8)
     grad_tiles(9, 10, a_r, dqkv_r, 9)
     steps((7, 0))
-    grad_tiles(10, 12, a_r, dqkv_r, 9)
+    grad_tiles(10, 11, a_r, dqkv_r, 9)
+    grad_tile(11, a_r, dqkv_r[:, 2 * 256:3 * 256])
     steps((6, 1), (4, 2))
 
     def phase_e(s, _):
-        ps_forward(1, s)
         steps_at(s, [], [(8, 0), (7, 1), (3, 1)], [])
         ps_finish(1, s)
 
@@ -526,6 +558,10 @@
 
         chunks(lnb)
 
+        @pl.when(s + 1 < S)
+        def _():
+            ps_forward(1, s + 1)
+
         steps_at(
             s,
             [(5, 2), (1, 2)],
@@ -552,34 +588,38 @@
             vst[j + 1] = total
             cp_v(j + 1).start()
         else:
-            vout_ref[...] = total
+            vout_ref[0:8, :] = total
+            vout_ref[8:9, :] = loss_r[...]
 
     cp_v(0).start()
-    steps((8, 1), (7, 2))
+    steps((8, 1), (7, 2), (10, 0), (9, 1))
     step_v(0)
-    steps((10, 0), (9, 1), (8, 2))
+    steps((11, 0), (10, 1), (8, 2))
     for j in range(1, NBITS - 1):
         step_v(j)
-    steps((11, 0), (10, 1), (9, 2), (11, 1))
+    steps((12, 0), (11, 1), (12, 1), (9, 2), (10, 2))
     step_v(NBITS - 1)
-    steps((10, 2), (11, 2))
+    steps((11, 2), (12, 2))
+
     def drain(tile, _):
         for j in range(NBITS):
             cp_g(tile, j).wait_send()
         return 0
 
-    lax.fori_loop(0, T, drain, 0)
-
-
-def finish(loss_in, v_in, *refs):
+    lax.fori_loop(0, T - 1, drain, 0)
+    drain(T - 1, 0)
+    drain(T, 0)
+
+
+def finish(v_in, *refs):
     ins, refs = refs[:6], refs[6:]
     loss_o, ln1g_o, ln1b_o, bqv_o, bproj_o, ln2g_o, ln2b_o, bfc1_o, bfc2_o = refs[:9]
     outs, sem = refs[9:15], refs[15]
     moves = [pltpu.make_async_copy(src, dst, sem.at[i]) for i, (src, dst) in enumerate(zip(ins, outs))]
     for c in moves:
         c.start()
-    for i in range(loss_in.shape[0]):
-        loss_o[i] = loss_in[i]
+    for i in range(loss_o.shape[0]):
+        loss_o[i] = v_in[8, i]
     for j, ref in enumerate([ln1g_o, ln1b_o, bproj_o, ln2g_o, ln2b_o, bfc1_o, bfc2_o]):
         ref[...] = v_in[j]
     lw = bqv_o.shape[1]
@@ -611,11 +651,11 @@
     big = [
         ((rows, D), BF16), ((rows, D), F32), ((FW, CH), F32), ((CH, FW), F32), ((LW, CH), F32), ((3, CH, LW), F32),
     ]
-    out, tg, loss, vout, *grads = pl.pallas_call(
+    out, tg, vout, *grads = pl.pallas_call(
         functools.partial(kernel, cfg),
-        out_shape=[V(*big[0]), V(*big[1]), sds((S,), F32), V((8, D), F32)] + [V(*b) for b in big[2:]],
+        out_shape=[V(*big[0]), V(*big[1]), V((16, D), F32)] + [V(*b) for b in big[2:]],
         in_specs=[sm] + [vm] * 8 + [any_spec] * 7,
-        out_specs=[vm, vm, sm, vm] + [vm] * 4,
+        out_specs=[vm] * 7,
         scratch_shapes=[
             V((3, D, LW), BF16), V((LW, D), BF16), V((D, FW), BF16), V((FW, D), BF16),
             V((rows, D), BF16), V((rows, D), BF16),
@@ -624,8 +664,8 @@
             V((rows, D), BF16), V((rows, FW), BF16), V((rows, 3 * LW), BF16),
             V((S, SLOTS, HALF), BF16), V((S, SLOTS, HALF), BF16), V((2, S, 2, 2, SLOTS, HALF), BF16),
             V((T, n_dp, CH, 256), BF16), V((T, n_dp - 1, CH, 256), BF16),
-            V((8, D), F32), V((8, D), F32), V((8, 8, D), F32), V((NBITS, 8, D), F32), V((NBITS, 8, D), F32),
-            DMA((6 + S,)), DMA((2, S, 4)), DMA((2, S, 4)), DMA((T, NBITS)), DMA((T, NBITS)),
+            V((8, D), F32), V((8, HALF), F32), V((1, D), F32), V((8, 8, D), F32), V((NBITS, 8, D), F32), V((NBITS, 8, D), F32),
+            DMA((6 + S,)), DMA((2, S, 4)), DMA((2, S, 4)), DMA((T + 1, NBITS)), DMA((T + 1, NBITS)),
             DMA((NBITS,)), DMA((NBITS,)),
         ],
         compiler_params=pltpu.CompilerParams(
@@ -642,12 +682,12 @@
             finish,
             out_shape=[sds((S,), F32), vd, vd, sds((2, LW), F32), vd, vd, vd, sds((FW,), F32), vd]
             + [sds(*b) for b in big],
-            in_specs=[sm, vm] + [vm] * 6,
+            in_specs=[vm] * 7,
             out_specs=[sm] + [vm] * 8 + [any_spec] * 6,
             scratch_shapes=[DMA((6,))],
             compiler_params=pltpu.CompilerParams(vmem_limit_bytes=16 * 2**20),
             name="finish",
-        )(loss, vout, out, tg, *grads)
+        )(vout, out, tg, *grads)
     )
     return (
         out, loss, token_grad, g_ln1g, g_ln1b, g_wqkv.transpose(1, 0, 2), g_bqv, g_wproj, g_bproj, g_ln2g, g_ln2b,

time: 140 us -> 137 us (0.979)
  Pallas kernels: 139 us -> 136 us
    pallas_call x1, Pallas kernels: 135 us -> 132 us  [body(): pl.pallas_call(functools.partial(kernel, cfg), out_shape=[V(*big[0]), V(*...]
where the time goes in v4:
time: 137 us
  Pallas kernels  136 us (99%)
    pallas_call x1, Pallas kernels, body(): pl.pallas_call(functools.partial(kernel, cfg), out_shape=[V(*big[0]), V(*...  132 us
    pallas_call x1, Pallas kernels, body(): pl.pallas_call(finish, out_shape=[sds((S,), F32), vd, vd, sds((2, LW), F3...  3.74 us

profile of v4, /device:TPU:0, one launch (start us, length us, event | category | flops | bytes accessed | tf_op | source)
XLA Modules:
  0.0 136.6 jit_solution(11835674464573217057)
XLA Ops:
  0.7 132.1 %layer.1 = (bf16[960,1024]{1,0:T(8,128)(2,1)S(1)}, f32[960,1024]{1,0:T(8,128)S(1)}, f32[16,1024]{1,0:T(8,128)S(1)}, f32[1024,128]{1,0:T(8,128)S(1)}, f32[128,102...) custom-call(s32[24]{0:T(128)} %kept_ref.1, bf16[1024]{0:T(1024)(128)(2,1)} %ln1g_in.1, ...), custom_call_target="tpu_custom_call" | custom-call | tf_op jit(solution)/shard_map/layer/pallas_call | solution.py:654
  132.7 3.7 %finish.1 = (f32[3]{0:T(128)}, f32[1024]{0:T(1024)}, f32[1024]{0:T(1024)}, f32[2,256]{1,0:T(2,128)}, f32[1024]{0:T(1024)}, /*index=5*/f32[1024]{0:T(1024)}, f32[...) custom-call(f32[16,1024]{1,0:T(8,128)S(1)} %get-tuple-element.37.v_i, ...), custom_call_target="tpu_custom_call" | custom-call | tf_op jit(solution)/shard_map/finish/pallas_call | solution.py:681

commit v5 on v4

--- a/solution.py
+++ b/solution.py
@@ -240,8 +240,17 @@
         val = mm(lhs[...], rhs, TN).astype(BF16)
         for d in range(NDP):
             gs[tile, place(d, f)] = val[d * CH:(d + 1) * CH]
-        cp_g(tile, 0).start()
-        if isinstance(tile, int) and tile == T - 1:
+        if isinstance(tile, int):
+            cp_g(tile, 0).start()
+            return
+
+        @pl.when(tile < T - 1)
+        def _():
+            cp_g(tile, 0).start()
+
+        @pl.when(tile == T - 1)
+        def _():
+            cp_g(T - 1, 0).start()
             cp_g(T, 0).start()
 
     def grad_tiles(first, last, lhs, rhs, skip=0):
@@ -504,15 +513,15 @@
         steps_at(
             s,
             [(0, 0)],
-            [(4, 0), (3, 0), (0, 1)],
-            [(5, 0), (4, 1), (1, 1), (0, 2)],
+            [(0, 1), (4, 0)],
+            [(5, 0), (4, 1)],
         )
         lax.fori_loop(0, npair, pair, 0, unroll=True)
         steps_at(
             s,
-            [(1, 0), (2, 0)],
-            [(2, 1)],
-            [(6, 0), (5, 1), (2, 2)],
+            [(2, 0)],
+            [(3, 0), (2, 1)],
+            [(6, 0), (5, 1)],
         )
         @pl.when(s + 1 < S)
         def _():
@@ -533,15 +542,21 @@
         return 0
 
     lax.fori_loop(0, S, phase_d, 0)
-    grad_tiles(8, 9, sl_r, heads_r, 8)
-    grad_tiles(9, 10, a_r, dqkv_r, 9)
-    steps((7, 0))
-    grad_tiles(10, 11, a_r, dqkv_r, 9)
-    grad_tile(11, a_r, dqkv_r[:, 2 * 256:3 * 256])
-    steps((6, 1), (4, 2))
+    grad_tile(8, sl_r, heads_r[...])
+
+    def attn_tile(k, _):
+        grad_tile(k, a_r, dqkv_r[:, pl.ds(pl.multiple_of((k - 9) * 256, 256), 256)])
+
+        @pl.when(k == 9)
+        def _():
+            steps((7, 0))
+
+        return 0
+
+    lax.fori_loop(9, 12, attn_tile, 0)
+    steps((1, 0), (6, 1))
 
     def phase_e(s, _):
-        steps_at(s, [], [(8, 0), (7, 1), (3, 1)], [])
         ps_finish(1, s)
 
         def lnb(i, _):
@@ -564,9 +579,9 @@
 
         steps_at(
             s,
-            [(5, 2), (1, 2)],
-            [(6, 2)],
-            [(9, 0), (3, 2)],
+            [(0, 2), (3, 1)],
+            [(2, 2), (7, 1)],
+            [],
         )
         return 0
 
@@ -592,14 +607,14 @@
             vout_ref[8:9, :] = loss_r[...]
 
     cp_v(0).start()
-    steps((8, 1), (7, 2), (10, 0), (9, 1))
+    steps((8, 0), (4, 2), (5, 2), (9, 0), (8, 1))
     step_v(0)
-    steps((11, 0), (10, 1), (8, 2))
+    steps((6, 2), (10, 0), (9, 1), (3, 2), (7, 2), (11, 0), (10, 1), (12, 0))
     for j in range(1, NBITS - 1):
         step_v(j)
-    steps((12, 0), (11, 1), (12, 1), (9, 2), (10, 2))
+    steps((11, 1), (8, 2), (1, 1), (12, 1))
     step_v(NBITS - 1)
-    steps((11, 2), (12, 2))
+    steps((9, 2), (10, 2), (11, 2), (1, 2), (12, 2))
 
     def drain(tile, _):
         for j in range(NBITS):
@@ -614,14 +629,16 @@
 def finish(v_in, *refs):
     ins, refs = refs[:6], refs[6:]
     loss_o, ln1g_o, ln1b_o, bqv_o, bproj_o, ln2g_o, ln2b_o, bfc1_o, bfc2_o = refs[:9]
-    outs, sem = refs[9:15], refs[15]
+    outs, sem, mids = refs[9:15], refs[15], refs[16:]
     moves = [pltpu.make_async_copy(src, dst, sem.at[i]) for i, (src, dst) in enumerate(zip(ins, outs))]
     for c in moves:
         c.start()
     for i in range(loss_o.shape[0]):
         loss_o[i] = v_in[8, i]
-    for j, ref in enumerate([ln1g_o, ln1b_o, bproj_o, ln2g_o, ln2b_o, bfc1_o, bfc2_o]):
-        ref[...] = v_in[j]
+    for j, (mid, ref) in enumerate(zip(mids, [ln1g_o, ln1b_o, bproj_o, ln2g_o, ln2b_o, bfc1_o, bfc2_o])):
+        mid[...] = v_in[j]
+        moves.append(pltpu.make_async_copy(mid, ref, sem.at[6 + j]))
+        moves[-1].start()
     lw = bqv_o.shape[1]
     bqv_o[0:1, :] = v_in[7:8, 0:lw]
     bqv_o[1:2, :] = v_in[7:8, lw:2 * lw]
@@ -683,8 +700,8 @@
             out_shape=[sds((S,), F32), vd, vd, sds((2, LW), F32), vd, vd, vd, sds((FW,), F32), vd]
             + [sds(*b) for b in big],
             in_specs=[vm] * 7,
-            out_specs=[sm] + [vm] * 8 + [any_spec] * 6,
-            scratch_shapes=[DMA((6,))],
+            out_specs=[sm, any_spec, any_spec, vm] + [any_spec] * 11,
+            scratch_shapes=[DMA((13,))] + [V((D,), F32)] * 5 + [V((FW,), F32), V((D,), F32)],
             compiler_params=pltpu.CompilerParams(vmem_limit_bytes=16 * 2**20),
             name="finish",
         )(vout, out, tg, *grads)

time: 137 us -> 135 us (0.985)
  Pallas kernels: 136 us -> 134 us
    pallas_call x1, Pallas kernels: 132 us -> 130 us  [body(): pl.pallas_call(functools.partial(kernel, cfg), out_shape=[V(*big[0]), V(*...]
where the time goes in v5:
time: 135 us
  Pallas kernels  134 us (99%)
    pallas_call x1, Pallas kernels, body(): pl.pallas_call(functools.partial(kernel, cfg), out_shape=[V(*big[0]), V(*...  130 us
    pallas_call x1, Pallas kernels, body(): pl.pallas_call(finish, out_shape=[sds((S,), F32), vd, vd, sds((2, LW), F3...  3.76 us

profile of v5, /device:TPU:0, one launch (start us, length us, event | category | flops | bytes accessed | tf_op | source)
XLA Modules:
  0.0 135.0 jit_solution(8251137185065942141)
XLA Ops:
  0.7 130.4 %layer.1 = (bf16[960,1024]{1,0:T(8,128)(2,1)S(1)}, f32[960,1024]{1,0:T(8,128)S(1)}, f32[16,1024]{1,0:T(8,128)S(1)}, f32[1024,128]{1,0:T(8,128)S(1)}, f32[128,102...) custom-call(s32[24]{0:T(128)} %kept_ref.1, bf16[1024]{0:T(1024)(128)(2,1)} %ln1g_in.1, ...), custom_call_target="tpu_custom_call" | custom-call | tf_op jit(solution)/shard_map/layer/pallas_call | solution.py:671
  131.1 3.8 %finish.1 = (f32[3]{0:T(128)}, f32[1024]{0:T(1024)}, f32[1024]{0:T(1024)}, f32[2,256]{1,0:T(2,128)}, f32[1024]{0:T(1024)}, /*index=5*/f32[1024]{0:T(1024)}, f32[...) custom-call(f32[16,1024]{1,0:T(8,128)S(1)} %get-tuple-element.37.v_i, ...), custom_call_target="tpu_custom_call" | custom-call | tf_op jit(solution)/shard_map/finish/pallas_call | solution.py:698

commit v6 on v5

--- a/solution.py
+++ b/solution.py
@@ -35,13 +35,13 @@
 
 def kernel(
     cfg,
-    kept_ref, ln1g_in, ln1b_in, bproj_in, ln2g_in, ln2b_in, bfc1_in, bfc2_in, bqv_in,
+    kept_in, ln1g_in, ln1b_in, bproj_in, ln2g_in, ln2b_in, bfc1_in, bfc2_in, bqv_in,
     tok_in, tea_in, og_in, wqkv_in, wproj_in, wfc1_in, wfc2_in,
     tea, seed_r, vout_ref, gfc2_r, gfc1_r, gproj_r, gqkv_r,
     wqkv, wproj, wfc1, wfc2, tok, og,
     a_r, qkv_r, heads_r, c_r, h1_r, act_r, gp_r, sl_r, dpre_r, dqkv_r,
     core_s, core_r, tot, gs, rb, vec_ref, lacc, loss_r, vacc, vst, vrc,
-    in_sem, ps_s, ps_r, g_s, g_r, v_s, v_r,
+    v1_ln1g, v1_ln1b, v1_bproj, v1_ln2g, v1_ln2b, v1_bfc1, v1_bfc2, v1_bqv, kept_ref, in_sem, ps_s, ps_r, px_r, g_s, g_r, v_s, v_r,
 ):
     S, NDP, NBITS, CH, FW = cfg
     LW = wproj.shape[0]
@@ -58,16 +58,12 @@
     def flip(b):
         return (dp + (1 << b) * (1 - 2 * bits[b]), t)
 
-    bar = pltpu.get_barrier_semaphore()
-    for peer in [sib, xn] + [flip(b) for b in range(NBITS)]:
-        pl.semaphore_signal(bar, inc=1, device_id=peer, device_id_type=MESH)
-
     def in_copy(i, src, dst):
         return pltpu.make_async_copy(src, dst, in_sem.at[i])
 
     def tok_copy(s):
         rows = pl.ds(pl.multiple_of(s * R, 64), R)
-        return pltpu.make_async_copy(tok_in.at[rows, :], tok.at[rows, :], in_sem.at[6 + s])
+        return pltpu.make_async_copy(tok_in.at[rows, :], tok.at[rows, :], in_sem.at[15 + s])
 
     ins = [
         in_copy(0, wqkv_in, wqkv),
@@ -77,19 +73,40 @@
         in_copy(4, tea_in, tea),
         in_copy(5, og_in, og),
     ]
+    v1 = [v1_ln1g, v1_ln1b, v1_bproj, v1_ln2g, v1_ln2b, v1_bfc1, v1_bfc2]
+    small = [
+        in_copy(6 + i, src, dst)
+        for i, (src, dst) in enumerate(zip([ln1g_in, ln1b_in, bproj_in, ln2g_in, ln2b_in, bfc1_in, bfc2_in], v1))
+    ]
+    bqv_copy, kept_copy = in_copy(13, bqv_in, v1_bqv), in_copy(14, kept_in, kept_ref)
     tok_copy(0).start()
+    kept_copy.start()
+    small[0].start()
+    small[1].start()
+    bqv_copy.start()
     ins[0].start()
     ins[1].start()
-    for j, ref in enumerate([ln1g_in, ln1b_in, bproj_in, ln2g_in, ln2b_in, bfc1_in, bfc2_in]):
-        vec_ref[j:j + 1, :] = ref[...].astype(F32).reshape(1, ref.shape[0])
+    for c in small[2:]:
+        c.start()
+
+    bar = pltpu.get_barrier_semaphore()
+    for peer in [sib, xn] + [flip(b) for b in range(NBITS)]:
+        pl.semaphore_signal(bar, inc=1, device_id=peer, device_id_type=MESH)
+
+    vacc[...] = jnp.zeros_like(vacc)
     vec_ref[7:8, :] = jnp.zeros((1, D), F32)
-    bqv = bqv_in[...].astype(F32)
+
+    def vec_rows(first, last):
+        for j in range(first, last):
+            small[j].wait()
+            vec_ref[j:j + 1, :] = v1[j][...].astype(F32).reshape(1, v1[j].shape[0])
+
+    vec_rows(0, 2)
+    bqv_copy.wait()
+    bqv = v1_bqv[...].astype(F32)
     vec_ref[7:8, 0:LW] = bqv[0:1]
     vec_ref[7:8, 2 * LW:3 * LW] = bqv[1:2]
-    vacc[...] = jnp.zeros_like(vacc)
-    count = lax.fori_loop(
-        0, kept_ref.shape[0], lambda i, acc: acc + (kept_ref[i] + BUFFER).astype(F32), jnp.float32(0.0)
-    )
+    kept_copy.wait()
 
     def length(s):
         return kept_ref[dp * S + s] + BUFFER
@@ -120,7 +137,7 @@
     def cp(p, s, kind, src, dst, dev):
         return pltpu.make_async_remote_copy(
             src_ref=src, dst_ref=dst,
-            send_sem=ps_s.at[p, s, kind], recv_sem=ps_r.at[p, s, kind],
+            send_sem=ps_s.at[s, kind], recv_sem=px_r.at[p, s] if kind == 1 else ps_r.at[s, kind // 2 + kind // 3],
             device_id=dev, device_id_type=MESH,
         )
 
@@ -231,7 +248,7 @@
         first = base(f, j) + (1 - stage_bit(f, j)) * n
         return pltpu.make_async_remote_copy(
             src_ref=gs.at[at, pl.ds(first, n), :, cols], dst_ref=rb.at[at, land(j):land(j) + n, :, cols],
-            send_sem=g_s.at[tile, j], recv_sem=g_r.at[tile, j],
+            send_sem=g_s.at[tile], recv_sem=g_r.at[tile, j],
             device_id=stage_peer(f, j), device_id_type=MESH,
         )
 
@@ -273,6 +290,7 @@
                 return 0
 
             lax.fori_loop(0, n, add, 0)
+            cp_g(tile, j).wait_send()
             cp_g(tile, j + 1).start()
             return
         val = gs[at, mine, :, cols].astype(F32) + rb[at, land(j), :, cols].astype(F32)
@@ -358,6 +376,11 @@
     lax.fori_loop(0, S, phase_a, 0)
 
     ps_forward(0, 0)
+
+    vec_rows(2, 7)
+    count = lax.fori_loop(
+        0, kept_ref.shape[0], lambda i, acc: acc + (kept_ref[i] + BUFFER).astype(F32), jnp.float32(0.0)
+    )
 
     ins[2].wait()
     ins[3].wait()
@@ -617,8 +640,7 @@
     steps((9, 2), (10, 2), (11, 2), (1, 2), (12, 2))
 
     def drain(tile, _):
-        for j in range(NBITS):
-            cp_g(tile, j).wait_send()
+        cp_g(tile, NBITS - 1).wait_send()
         return 0
 
     lax.fori_loop(0, T - 1, drain, 0)
@@ -633,15 +655,19 @@
     moves = [pltpu.make_async_copy(src, dst, sem.at[i]) for i, (src, dst) in enumerate(zip(ins, outs))]
     for c in moves:
         c.start()
+    loss_s, bqv_s, mids = mids[0], mids[1], mids[2:]
     for i in range(loss_o.shape[0]):
-        loss_o[i] = v_in[8, i]
+        loss_s[i] = v_in[8, i]
     for j, (mid, ref) in enumerate(zip(mids, [ln1g_o, ln1b_o, bproj_o, ln2g_o, ln2b_o, bfc1_o, bfc2_o])):
         mid[...] = v_in[j]
         moves.append(pltpu.make_async_copy(mid, ref, sem.at[6 + j]))
         moves[-1].start()
     lw = bqv_o.shape[1]
-    bqv_o[0:1, :] = v_in[7:8, 0:lw]
-    bqv_o[1:2, :] = v_in[7:8, lw:2 * lw]
+    bqv_s[0:1, :] = v_in[7:8, 0:lw]
+    bqv_s[1:2, :] = v_in[7:8, lw:2 * lw]
+    for j, (mid, ref) in enumerate(((loss_s, loss_o), (bqv_s, bqv_o))):
+        moves.append(pltpu.make_async_copy(mid, ref, sem.at[13 + j]))
+        moves[-1].start()
     for c in moves:
         c.wait()
 
@@ -671,7 +697,7 @@
     out, tg, vout, *grads = pl.pallas_call(
         functools.partial(kernel, cfg),
         out_shape=[V(*big[0]), V(*big[1]), V((16, D), F32)] + [V(*b) for b in big[2:]],
-        in_specs=[sm] + [vm] * 8 + [any_spec] * 7,
+        in_specs=[any_spec] * 16,
         out_specs=[vm] * 7,
         scratch_shapes=[
             V((3, D, LW), BF16), V((LW, D), BF16), V((D, FW), BF16), V((FW, D), BF16),
@@ -682,7 +708,8 @@
             V((S, SLOTS, HALF), BF16), V((S, SLOTS, HALF), BF16), V((2, S, 2, 2, SLOTS, HALF), BF16),
             V((T, n_dp, CH, 256), BF16), V((T, n_dp - 1, CH, 256), BF16),
             V((8, D), F32), V((8, HALF), F32), V((1, D), F32), V((8, 8, D), F32), V((NBITS, 8, D), F32), V((NBITS, 8, D), F32),
-            DMA((6 + S,)), DMA((2, S, 4)), DMA((2, S, 4)), DMA((T + 1, NBITS)), DMA((T + 1, NBITS)),
+            V((D,), BF16), V((D,), BF16), V((D,), BF16), V((D,), BF16), V((D,), BF16), V((FW,), BF16), V((D,), BF16),
+            V((2, LW), BF16), pltpu.SMEM((kept.shape[0],), jnp.int32), DMA((15 + S,)), DMA((S, 4)), DMA((S, 3)), DMA((2, S)), DMA((T + 1,)), DMA((T + 1, NBITS)),
             DMA((NBITS,)), DMA((NBITS,)),
         ],
         compiler_params=pltpu.CompilerParams(
@@ -700,8 +727,8 @@
             out_shape=[sds((S,), F32), vd, vd, sds((2, LW), F32), vd, vd, vd, sds((FW,), F32), vd]
             + [sds(*b) for b in big],
             in_specs=[vm] * 7,
-            out_specs=[sm, any_spec, any_spec, vm] + [any_spec] * 11,
-            scratch_shapes=[DMA((13,))] + [V((D,), F32)] * 5 + [V((FW,), F32), V((D,), F32)],
+            out_specs=[any_spec] * 15,
+            scratch_shapes=[DMA((15,)), pltpu.SMEM((S,), F32), V((2, LW), F32)] + [V((D,), F32)] * 5 + [V((FW,), F32), V((D,), F32)],
             compiler_params=pltpu.CompilerParams(vmem_limit_bytes=16 * 2**20),
             name="finish",
         )(vout, out, tg, *grads)

time: 135 us -> 133 us (0.985)
  Pallas kernels: 134 us -> 132 us
where the time goes in v6:
time: 133 us
  Pallas kernels  132 us (99%)
    pallas_call x1, Pallas kernels, body(): pl.pallas_call(functools.partial(kernel, cfg), out_shape=[V(*big[0]), V(*...  129 us
    pallas_call x1, Pallas kernels, body(): pl.pallas_call(finish, out_shape=[sds((S,), F32), vd, vd, sds((2, LW), F3...  3.21 us

profile of v6, /device:TPU:0, one launch (start us, length us, event | category | flops | bytes accessed | tf_op | source)
XLA Modules:
  0.0 133.1 jit_solution(7887293468208459744)
XLA Ops:
  0.7 129.1 %layer.1 = (bf16[960,1024]{1,0:T(8,128)(2,1)S(1)}, f32[960,1024]{1,0:T(8,128)S(1)}, f32[16,1024]{1,0:T(8,128)S(1)}, f32[1024,128]{1,0:T(8,128)S(1)}, f32[128,102...) custom-call(s32[24]{0:T(128)} %kept_in.1, bf16[1024]{0:T(1024)(128)(2,1)} %ln1g_in.1, ...), custom_call_target="tpu_custom_call" | custom-call | tf_op jit(solution)/shard_map/layer/pallas_call | solution.py:697
  129.7 3.2 %finish.1 = (f32[3]{0:T(128)}, f32[1024]{0:T(1024)}, f32[1024]{0:T(1024)}, f32[2,256]{1,0:T(2,128)}, f32[1024]{0:T(1024)}, /*index=5*/f32[1024]{0:T(1024)}, f32[...) custom-call(f32[16,1024]{1,0:T(8,128)S(1)} %get-tuple-element.37.v_i, ...), custom_call_target="tpu_custom_call" | custom-call | tf_op jit(solution)/shard_map/finish/pallas_call | solution.py:725

commit v7 on v6

--- a/solution.py
+++ b/solution.py
@@ -134,45 +134,59 @@
         r = lax.rsqrt(var + EPS)
         return off * r, r
 
-    def cp(p, s, kind, src, dst, dev):
+    HR = R // 2
+
+    def pieces(p):
+        return (0, 1)
+
+    def piece(ref, r):
+        return ref if r is None else ref.at[pl.ds(r * HR, HR)]
+
+    def cp(s, send, recv, src, dst, dev):
         return pltpu.make_async_remote_copy(
-            src_ref=src, dst_ref=dst,
-            send_sem=ps_s.at[s, kind], recv_sem=px_r.at[p, s] if kind == 1 else ps_r.at[s, kind // 2 + kind // 3],
-            device_id=dev, device_id_type=MESH,
+            src_ref=src, dst_ref=dst, send_sem=ps_s.at[s, send], recv_sem=recv, device_id=dev, device_id_type=MESH
         )
 
-    def cp_core(p, s):
-        return cp(p, s, 0, core_s.at[s], core_r.at[s], sib)
-
-    def cp_x(p, s):
-        ref = tot.at[p, s, lo, hi]
-        return cp(p, s, 1, ref, ref, xn)
+    def cp_core(p, s, r):
+        return cp(s, 6 * r, ps_r.at[s, 4 * r], piece(core_s.at[s], r), piece(core_r.at[s], r), sib)
+
+    def cp_x(p, s, r):
+        ref = piece(tot.at[p, s, lo, hi], r)
+        return cp(s, 4 if r == 1 else 1, px_r.at[2 * r + p, s], ref, ref, xn)
 
     def cp_f1(p, s):
         ref = tot.at[p, s, lo, hi]
-        return cp(p, s, 2, ref, ref, sib)
-
-    def cp_f2(p, s):
-        ref = tot.at[p, s, lo, 1 - hi]
-        return cp(p, s, 3, ref, ref, sib)
+        return cp(s, 2, ps_r.at[s, 1], ref, ref, sib)
+
+    def cp_f2(p, s, r):
+        ref = piece(tot.at[p, s, lo, 1 - hi], r)
+        return cp(s, 5 if r == 1 else 3, ps_r.at[s, 3 if r == 1 else 2], ref, ref, sib)
 
     def ps_start(p, s, part):
         core_s[s] = part(1 - lo).astype(BF16)
-        cp_core(p, s).start()
+        for r in pieces(p):
+            cp_core(p, s, r).start()
         own = part(lo).astype(BF16).astype(F32)
-        cp_core(p, s).wait_recv()
-        tot[p, s, lo, hi] = (own + core_r[s].astype(F32)).astype(BF16)
-        cp_x(p, s).start()
+        for r in pieces(p):
+            rr = pl.ds(r * HR, HR)
+            cp_core(p, s, r).wait_recv()
+            tot[p, s, lo, hi, rr] = (own[r * HR:(r + 1) * HR] + core_r[s, rr].astype(F32)).astype(BF16)
+            cp_x(p, s, r).start()
         cp_f1(p, s).start()
 
+    def ps_pass_on(p, s, r):
+        cp_x(p, s, r).wait()
+        cp_f2(p, s, r).start()
+
     def ps_forward(p, s):
-        cp_core(p, s).wait_send()
-        cp_x(p, s).wait()
-        cp_f2(p, s).start()
+        for r in pieces(p):
+            cp_core(p, s, r).wait_send()
+            ps_pass_on(p, s, r)
 
     def ps_finish(p, s):
         cp_f1(p, s).wait()
-        cp_f2(p, s).wait()
+        for r in pieces(p):
+            cp_f2(p, s, r).wait()
 
     def ps_total(p, s, i):
         rr = loc(i)
@@ -253,8 +267,11 @@
         )
 
     def grad_tile(tile, lhs, rhs):
+        store_tile(tile, mm(lhs[...], rhs, TN))
+
+    def store_tile(tile, val):
         f = swapped(tile)
-        val = mm(lhs[...], rhs, TN).astype(BF16)
+        val = val.astype(BF16)
         for d in range(NDP):
             gs[tile, place(d, f)] = val[d * CH:(d + 1) * CH]
         if isinstance(tile, int):
@@ -432,7 +449,7 @@
     def phase_c(s, _):
         lacc[...] = jnp.zeros_like(lacc)
 
-        def fin(h):
+        def fin(h, r=None):
             hc = half_cols(h)
 
             def one(i, _):
@@ -448,20 +465,37 @@
                 vacc[6, :, hc] += fold8(seed)
                 return 0
 
-            chunks(one)
-
-        fin(lo)
-        ps_finish(1, s)
-        fin(1 - lo)
-        here = (lax.broadcasted_iota(jnp.int32, (1, D), 1) == s).astype(F32)
-        loss_r[...] += here * (jnp.sum(lacc[...]) * loss_scale)
+            n = R // RB
+            first, last = (0, n) if r is None else (r * n // 2, (r + 1) * n // 2)
+            lax.fori_loop(first, last, one, 0, unroll=5)
+
+        @pl.when(s < S - 1)
+        def _():
+            fin(lo)
+            ps_finish(1, s)
+            fin(1 - lo)
+
+        @pl.when(s == S - 1)
+        def _():
+            last = S - 1
+            for r in pieces(1):
+                cp_core(1, last, r).wait_send()
+            ps_pass_on(1, last, 0)
+            fin(lo, 0)
+            cp_f1(1, last).wait()
+            cp_f2(1, last, 0).wait()
+            fin(1 - lo, 0)
+            ps_pass_on(1, last, 1)
+            fin(lo, 1)
+            cp_f2(1, last, 1).wait()
+            fin(1 - lo, 1)
+
         rs = seq_rows(s)
         sv = sl_r[rs, :]
 
         @pl.when(s == S - 1)
         def _():
             grad_tiles(0, 2, sl_r, act_r)
-
 
         def dact(j, _):
             cs = pl.ds(pl.multiple_of(j * 256, 256), 256)
@@ -474,7 +508,10 @@
         lax.fori_loop(0, FW // 256, dact, 0)
         ps_start(0, s, lambda h: mm(dpre_r[rs, :], wfc1[half_cols(h), :], NT))
 
-        @pl.when(s + 1 < S)
+        here = (lax.broadcasted_iota(jnp.int32, (1, D), 1) == s).astype(F32)
+        loss_r[...] += here * (jnp.sum(lacc[...]) * loss_scale)
+
+        @pl.when(s + 1 < S - 1)
         def _():
             ps_forward(1, s + 1)
 
@@ -632,7 +669,7 @@
     cp_v(0).start()
     steps((8, 0), (4, 2), (5, 2), (9, 0), (8, 1))
     step_v(0)
-    steps((6, 2), (10, 0), (9, 1), (3, 2), (7, 2), (11, 0), (10, 1), (12, 0))
+    steps((6, 2), (10, 0), (9, 1), (3, 2), (7, 2), (11, 0), (12, 0), (10, 1))
     for j in range(1, NBITS - 1):
         step_v(j)
     steps((11, 1), (8, 2), (1, 1), (12, 1))
@@ -709,7 +746,7 @@
             V((T, n_dp, CH, 256), BF16), V((T, n_dp - 1, CH, 256), BF16),
             V((8, D), F32), V((8, HALF), F32), V((1, D), F32), V((8, 8, D), F32), V((NBITS, 8, D), F32), V((NBITS, 8, D), F32),
             V((D,), BF16), V((D,), BF16), V((D,), BF16), V((D,), BF16), V((D,), BF16), V((FW,), BF16), V((D,), BF16),
-            V((2, LW), BF16), pltpu.SMEM((kept.shape[0],), jnp.int32), DMA((15 + S,)), DMA((S, 4)), DMA((S, 3)), DMA((2, S)), DMA((T + 1,)), DMA((T + 1, NBITS)),
+            V((2, LW), BF16), pltpu.SMEM((kept.shape[0],), jnp.int32), DMA((15 + S,)), DMA((S, 7)), DMA((S, 5)), DMA((4, S)), DMA((T + 1,)), DMA((T + 1, NBITS)),
             DMA((NBITS,)), DMA((NBITS,)),
         ],
         compiler_params=pltpu.CompilerParams(

time: 133 us -> 133 us (level)
  no operation moved by 1% of the time
where the time goes in v7:
time: 133 us
  Pallas kernels  132 us (99%)
    pallas_call x1, Pallas kernels, body(): pl.pallas_call(functools.partial(kernel, cfg), out_shape=[V(*big[0]), V(*...  129 us
    pallas_call x1, Pallas kernels, body(): pl.pallas_call(finish, out_shape=[sds((S,), F32), vd, vd, sds((2, LW), F3...  3.21 us

profile of v7, /device:TPU:0, one launch (start us, length us, event | category | flops | bytes accessed | tf_op | source)
XLA Modules:
  0.0 132.8 jit_solution(934541948899386497)
XLA Ops:
  0.7 128.7 %layer.1 = (bf16[960,1024]{1,0:T(8,128)(2,1)S(1)}, f32[960,1024]{1,0:T(8,128)S(1)}, f32[16,1024]{1,0:T(8,128)S(1)}, f32[1024,128]{1,0:T(8,128)S(1)}, f32[128,102...) custom-call(s32[24]{0:T(128)} %kept_in.1, bf16[1024]{0:T(1024)(128)(2,1)} %ln1g_in.1, ...), custom_call_target="tpu_custom_call" | custom-call | tf_op jit(solution)/shard_map/layer/pallas_call | solution.py:734
  129.4 3.2 %finish.1 = (f32[3]{0:T(128)}, f32[1024]{0:T(1024)}, f32[1024]{0:T(1024)}, f32[2,256]{1,0:T(2,128)}, f32[1024]{0:T(1024)}, /*index=5*/f32[1024]{0:T(1024)}, f32[...) custom-call(f32[16,1024]{1,0:T(8,128)S(1)} %get-tuple-element.37.v_i, ...), custom_call_target="tpu_custom_call" | custom-call | tf_op jit(solution)/shard_map/finish/pallas_call | solution.py:762

commit v8 on v6

--- a/solution.py
+++ b/solution.py
@@ -119,7 +119,7 @@
         return pl.ds(pl.multiple_of(s * R, 64), R)
 
     def chunks(fn, init=0):
-        return lax.fori_loop(0, R // RB, fn, init, unroll=5)
+        return lax.fori_loop(0, R // RB, fn, init, unroll=10)
 
     def blk(s, i):
         return pl.ds(pl.multiple_of(s * R + i * RB, RB), RB)
@@ -341,8 +341,6 @@
                 return 0
 
             lax.fori_loop(1, S, tok_start, 0)
-            for c in ins[2:]:
-                c.start()
 
         rs = seq_rows(s)
         av = a_r[rs, :]
@@ -371,6 +369,12 @@
             pl.semaphore_wait(bar, 2 + NBITS)
 
         ps_start(0, s, lambda h: mm(hv, wproj[:, half_cols(h)], NN))
+
+        @pl.when(s == 0)
+        def _():
+            for c in ins[2:]:
+                c.start()
+
         return 0
 
     lax.fori_loop(0, S, phase_a, 0)

time: 133 us -> 133 us (level)
  no operation moved by 1% of the time
where the time goes in v8:
time: 133 us
  Pallas kernels  132 us (99%)
    pallas_call x1, Pallas kernels, body(): pl.pallas_call(functools.partial(kernel, cfg), out_shape=[V(*big[0]), V(*...  129 us
    pallas_call x1, Pallas kernels, body(): pl.pallas_call(finish, out_shape=[sds((S,), F32), vd, vd, sds((2, LW), F3...  3.21 us

profile of v8, /device:TPU:0, one launch (start us, length us, event | category | flops | bytes accessed | tf_op | source)
XLA Modules:
  0.0 133.1 jit_solution(1245235879060909153)
XLA Ops:
  0.7 129.1 %layer.1 = (bf16[960,1024]{1,0:T(8,128)(2,1)S(1)}, f32[960,1024]{1,0:T(8,128)S(1)}, f32[16,1024]{1,0:T(8,128)S(1)}, f32[1024,128]{1,0:T(8,128)S(1)}, f32[128,102...) custom-call(s32[24]{0:T(128)} %kept_in.1, bf16[1024]{0:T(1024)(128)(2,1)} %ln1g_in.1, ...), custom_call_target="tpu_custom_call" | custom-call | tf_op jit(solution)/shard_map/layer/pallas_call | solution.py:701
  129.7 3.2 %finish.1 = (f32[3]{0:T(128)}, f32[1024]{0:T(1024)}, f32[1024]{0:T(1024)}, f32[2,256]{1,0:T(2,128)}, f32[1024]{0:T(1024)}, /*index=5*/f32[1024]{0:T(1024)}, f32[...) custom-call(f32[16,1024]{1,0:T(8,128)S(1)} %get-tuple-element.37.v_i, ...), custom_call_target="tpu_custom_call" | custom-call | tf_op jit(solution)/shard_map/finish/pallas_call | solution.py:729
